TPU v7x, 512 devices: a whole 4x4x16 slice. The times are simulated.
512 devices in a mesh: gx: 32 (over x, y, core), gy: 16 (over z).
Axes of the slice: x: 4, y: 4, z: 16, core: 2. Of those that a mesh axis runs over, the one named last changes fastest.
Arguments:
- basis_vec: float32 [16, 512, 4096], P(None, 'gx', 'gy'), may hold values from -6 to 6
- conductivity: float32 [16, 512, 4096], P(None, 'gx', 'gy'), may hold values from 0.2 to 5
- sign_vals: int32 [512, 4096], P('gx', 'gy'), may hold values from -1 to 1, as said below
- sample_cols: int32 [256], P('gy'), may hold values from 0 to 255, as said below
Outputs:
- precond: float32 [16, 512, 4096], P(None, 'gx', 'gy')
- image_vec: float32 [16, 512, 4096], P(None, 'gx', 'gy')
- sketch: float32 [16, 512, 16], P(None, 'gx')
Inputs may be any that keep to these rules, and one draw needn't show every extreme that they name: `sign_vals`: each entry is -1 or 1. `sample_cols`: the entries of each aligned block of 16 are distinct column offsets within one block of 256 columns.
All inputs are finite; a program needn't handle non-finite values.
Results may differ from a plain program's by a relative error of at most 0.0002.
Values sent between devices are 32-bit elements; how exact they have to be, the bound alone decides.
A program may use at most 64 MiB of HBM per device.

v0:
```python
import jax
import jax.numpy as jnp
from jax import lax
from jax.sharding import PartitionSpec as P

SWEEPS = 8


reaction = 0.5
lowest = 0.5
highest = 62.0
half_root = 0.7071067811865476


def extended(array, sides, width):
    for axis, dim in sides:
        devices, length = (lax.axis_size(axis), array.shape[dim])
        up = [(i, (i + 1) % devices) for i in range(devices - 1)]
        down = [(j, i) for i, j in up]
        last = lax.slice_in_dim(array, length - width, length, axis=dim)
        leading = lax.slice_in_dim(array, 0, width, axis=dim)
        before = lax.ppermute(last, axis, up)
        after = lax.ppermute(leading, axis, down)
        array = jnp.concatenate([before, array, after], axis=dim)
    return array


def partner_2(array, axis, stride):
    return lax.ppermute(array, axis, [(i, i ^ 1 << stride) for i in range(lax.axis_size(axis))])


def operate(values, conduct):
    padded = jnp.pad(values, ((1, 1), (0, 0), (0, 0)))
    centre_val = padded[1:-1, 1:-1, 1:-1]
    kappa_mid = conduct[1:-1, 1:-1, 1:-1]
    neighbours = (
        (padded[2:, 1:-1, 1:-1], conduct[2:, 1:-1, 1:-1]),
        (padded[:-2, 1:-1, 1:-1], conduct[:-2, 1:-1, 1:-1]),
        (padded[1:-1, 2:, 1:-1], conduct[1:-1, 2:, 1:-1]),
        (padded[1:-1, :-2, 1:-1], conduct[1:-1, :-2, 1:-1]),
        (padded[1:-1, 1:-1, 2:], conduct[1:-1, 1:-1, 2:]),
        (padded[1:-1, 1:-1, :-2], conduct[1:-1, 1:-1, :-2]),
    )
    summed = reaction * centre_val
    for near_value, near_kappa in neighbours:
        summed = summed + 0.5 * (kappa_mid + near_kappa) * (centre_val - near_value)
    return summed


def hartley_table(length):
    row_ids = jnp.arange(length, dtype=jnp.int32)[:, None]
    col_ids = jnp.arange(length, dtype=jnp.int32)[None, :]
    angles = (row_ids * col_ids % length).astype(jnp.float32) * (2.0 * jnp.pi / length)
    return (jnp.cos(angles) + jnp.sin(angles)) / jnp.sqrt(jnp.float32(length))


def per_device(basis_vec, conductivity, sign_vals, sample_cols):
    depth_cells, row_cells, col_cells = basis_vec.shape
    margin = 1
    conduct = extended(conductivity, (("gx", 1), ("gy", 2)), margin)
    conduct = jnp.pad(conduct, ((1, 1), (0, 0), (0, 0)))
    conduct_one = conduct

    def apply_rim(values):
        padded = extended(values, (("gx", 1), ("gy", 2)), 1)
        return operate(padded, conduct_one)

    middle = (highest + lowest) / 2.0
    spread = (highest - lowest) / 2.0
    sig_ratio = middle / spread
    rho_now = 1.0 / sig_ratio
    residual = basis_vec
    direction = residual * (1.0 / middle)
    precond = jnp.zeros_like(basis_vec)
    for sweep_no in range(SWEEPS):
        precond = precond + direction
        if sweep_no < SWEEPS - 1:
            residual = residual - apply_rim(direction)
            rho_next = 1.0 / (2.0 * sig_ratio - rho_now)
            direction = rho_next * rho_now * direction + 2.0 * rho_next / spread * residual
            rho_now = rho_next
    image_vec = apply_rim(precond)
    flipped = image_vec * sign_vals.astype(jnp.float32)[None]
    hartley_mat = hartley_table(row_cells)
    current = jnp.einsum("jk,dkc->djc", hartley_mat, flipped, precision=lax.Precision.HIGHEST)
    for section_bit in range(lax.axis_size("gx").bit_length() - 1):
        partner = partner_2(current, "gx", section_bit)
        upper_half = lax.axis_index("gx") >> section_bit & 1 == 1
        current = jnp.where(upper_half, partner - current, current + partner) * half_root
    picked = jnp.take(current, sample_cols, axis=2)
    sketch = lax.psum(picked, "gy")
    return (precond, image_vec, sketch)


def solution(mesh):
    in_specs = (P(None, "gx", "gy"), P(None, "gx", "gy"), P("gx", "gy"), P("gy"))
    out_specs = (P(None, "gx", "gy"), P(None, "gx", "gy"), P(None, "gx", None))
    return jax.shard_map(
        per_device, mesh=mesh, in_specs=in_specs, out_specs=out_specs, check_vma=False
    )
```

profile of v0, /device:TPU:24, one launch (start us, length us, event | category | flops | bytes accessed | tf_op | source)
XLA Modules:
  0.0 297.3 jit_solution(12451882532741742519)
XLA Ops:
  20.5 4.6 %collective-permute-start.6 = (f32[16,18,1]{2,1,0:T(8,128)S(1)}, f32[16,18,1]{2,1,0:T(8,128)S(1)}, u32[]{:S(2)}, u32[]{:S(2)}) collective-permute-start(f32[16,18,1]{2,1,0:T(8,128)S(1)} %get-tuple-element.39), channel_id=1, source_target_pairs={{0,1},{1,2},{2,3},{3,4},{4,5},{5,6},{6,7},{7,8},{8,9},{9,10},{10,1... | collective-permute-start | bytes 3464 | tf_op jit(solution)/shard_map/ppermute | solution.py:22
  30.0 4.5 %collective-permute-done.7 = f32[16,18,1]{2,1,0:T(8,128)S(1)} collective-permute-done((f32[16,18,1]{2,1,0:T(8,128)S(1)}, f32[16,18,1]{2,1,0:T(8,128)S(1)}, u32[]{:S(2)}, u32[]{:S(2)}) %collective-permute-start.7) | collective-permute-done | bytes 1184 | tf_op jit(solution)/shard_map/ppermute | solution.py:23
  44.1 4.8 %collective-permute-start.10 = (f32[16,18,1]{2,1,0:T(8,128)S(1)}, f32[16,18,1]{2,1,0:T(8,128)S(1)}, u32[]{:S(2)}, u32[]{:S(2)}) collective-permute-start(f32[16,18,1]{2,1,0:T(8,128)S(1)} %get-tuple-element.35), channel_id=1, source_target_pairs={{0,1},{1,2},{2,3},{3,4},{4,5},{5,6},{6,7},{7,8},{8,9},{9,10},{10,1... | collective-permute-start | bytes 3464 | tf_op jit(solution)/shard_map/ppermute | solution.py:22
  52.1 5.6 %collective-permute-done.11 = f32[16,18,1]{2,1,0:T(8,128)S(1)} collective-permute-done((f32[16,18,1]{2,1,0:T(8,128)S(1)}, f32[16,18,1]{2,1,0:T(8,128)S(1)}, u32[]{:S(2)}, u32[]{:S(2)}) %collective-permute-start.11) | collective-permute-done | bytes 1184 | tf_op jit(solution)/shard_map/ppermute | solution.py:23
  58.7 5.3 %collective-permute-start.12 = (f32[16,1,256]{2,1,0:T(1,128)S(1)}, f32[16,1,256]{2,1,0:T(1,128)S(1)}, u32[]{:S(2)}, u32[]{:S(2)}) collective-permute-start(f32[16,1,256]{2,1,0:T(1,128)S(1)} %get-tuple-element.50), channel_id=1, source_target_pairs={{0,16},{16,32},{32,48},{48,64},{64,80},{80,96},{96,112},{112,128},... | collective-permute-start | bytes 49160 | tf_op jit(solution)/shard_map/ppermute | solution.py:22
  68.0 5.1 %collective-permute-start.14 = (f32[16,18,1]{2,1,0:T(8,128)S(1)}, f32[16,18,1]{2,1,0:T(8,128)S(1)}, u32[]{:S(2)}, u32[]{:S(2)}) collective-permute-start(f32[16,18,1]{2,1,0:T(8,128)S(1)} %get-tuple-element.33), channel_id=1, source_target_pairs={{0,1},{1,2},{2,3},{3,4},{4,5},{5,6},{6,7},{7,8},{8,9},{9,10},{10,1... | collective-permute-start | bytes 3464 | tf_op jit(solution)/shard_map/ppermute | solution.py:22
  76.3 4.4 %collective-permute-done.15 = f32[16,18,1]{2,1,0:T(8,128)S(1)} collective-permute-done((f32[16,18,1]{2,1,0:T(8,128)S(1)}, f32[16,18,1]{2,1,0:T(8,128)S(1)}, u32[]{:S(2)}, u32[]{:S(2)}) %collective-permute-start.15) | collective-permute-done | bytes 1184 | tf_op jit(solution)/shard_map/ppermute | solution.py:23
  81.7 5.3 %collective-permute-start.16 = (f32[16,1,256]{2,1,0:T(1,128)S(1)}, f32[16,1,256]{2,1,0:T(1,128)S(1)}, u32[]{:S(2)}, u32[]{:S(2)}) collective-permute-start(f32[16,1,256]{2,1,0:T(1,128)S(1)} %get-tuple-element.48), channel_id=1, source_target_pairs={{0,16},{16,32},{32,48},{48,64},{64,80},{80,96},{96,112},{112,128},... | collective-permute-start | bytes 49160 | tf_op jit(solution)/shard_map/ppermute | solution.py:22
  98.1 4.4 %collective-permute-done.19 = f32[16,18,1]{2,1,0:T(8,128)S(1)} collective-permute-done((f32[16,18,1]{2,1,0:T(8,128)S(1)}, f32[16,18,1]{2,1,0:T(8,128)S(1)}, u32[]{:S(2)}, u32[]{:S(2)}) %collective-permute-start.19) | collective-permute-done | bytes 1184 | tf_op jit(solution)/shard_map/ppermute | solution.py:23
  103.5 5.1 %collective-permute-start.20 = (f32[16,1,256]{2,1,0:T(1,128)S(1)}, f32[16,1,256]{2,1,0:T(1,128)S(1)}, u32[]{:S(2)}, u32[]{:S(2)}) collective-permute-start(f32[16,1,256]{2,1,0:T(1,128)S(1)} %get-tuple-element.46), channel_id=1, source_target_pairs={{0,16},{16,32},{32,48},{48,64},{64,80},{80,96},{96,112},{112,128},... | collective-permute-start | bytes 49160 | tf_op jit(solution)/shard_map/ppermute | solution.py:22
  112.8 4.7 %collective-permute-start.22 = (f32[16,18,1]{2,1,0:T(8,128)S(1)}, f32[16,18,1]{2,1,0:T(8,128)S(1)}, u32[]{:S(2)}, u32[]{:S(2)}) collective-permute-start(f32[16,18,1]{2,1,0:T(8,128)S(1)} %get-tuple-element.29), channel_id=1, source_target_pairs={{0,1},{1,2},{2,3},{3,4},{4,5},{5,6},{6,7},{7,8},{8,9},{9,10},{10,1... | collective-permute-start | bytes 3464 | tf_op jit(solution)/shard_map/ppermute | solution.py:22
  126.2 5.3 %collective-permute-start.24 = (f32[16,1,256]{2,1,0:T(1,128)S(1)}, f32[16,1,256]{2,1,0:T(1,128)S(1)}, u32[]{:S(2)}, u32[]{:S(2)}) collective-permute-start(f32[16,1,256]{2,1,0:T(1,128)S(1)} %get-tuple-element.44), channel_id=1, source_target_pairs={{0,16},{16,32},{32,48},{48,64},{64,80},{80,96},{96,112},{112,128},... | collective-permute-start | bytes 49160 | tf_op jit(solution)/shard_map/ppermute | solution.py:22
  135.4 5.1 %collective-permute-start.26 = (f32[16,18,1]{2,1,0:T(8,128)S(1)}, f32[16,18,1]{2,1,0:T(8,128)S(1)}, u32[]{:S(2)}, u32[]{:S(2)}) collective-permute-start(f32[16,18,1]{2,1,0:T(8,128)S(1)} %get-tuple-element.27), channel_id=1, source_target_pairs={{0,1},{1,2},{2,3},{3,4},{4,5},{5,6},{6,7},{7,8},{8,9},{9,10},{10,1... | collective-permute-start | bytes 3464 | tf_op jit(solution)/shard_map/ppermute | solution.py:22
  143.7 4.4 %collective-permute-done.27 = f32[16,18,1]{2,1,0:T(8,128)S(1)} collective-permute-done((f32[16,18,1]{2,1,0:T(8,128)S(1)}, f32[16,18,1]{2,1,0:T(8,128)S(1)}, u32[]{:S(2)}, u32[]{:S(2)}) %collective-permute-start.27) | collective-permute-done | bytes 1184 | tf_op jit(solution)/shard_map/ppermute | solution.py:23
  149.2 5.3 %collective-permute-start.28 = (f32[16,1,256]{2,1,0:T(1,128)S(1)}, f32[16,1,256]{2,1,0:T(1,128)S(1)}, u32[]{:S(2)}, u32[]{:S(2)}) collective-permute-start(f32[16,1,256]{2,1,0:T(1,128)S(1)} %get-tuple-element.42), channel_id=1, source_target_pairs={{0,16},{16,32},{32,48},{48,64},{64,80},{80,96},{96,112},{112,128},... | collective-permute-start | bytes 49160 | tf_op jit(solution)/shard_map/ppermute | solution.py:22
  165.6 4.4 %collective-permute-done.31 = f32[16,18,1]{2,1,0:T(8,128)S(1)} collective-permute-done((f32[16,18,1]{2,1,0:T(8,128)S(1)}, f32[16,18,1]{2,1,0:T(8,128)S(1)}, u32[]{:S(2)}, u32[]{:S(2)}) %collective-permute-start.31) | collective-permute-done | bytes 1184 | tf_op jit(solution)/shard_map/ppermute | solution.py:23
  171.2 5.3 %collective-permute-start.32 = (f32[16,1,256]{2,1,0:T(1,128)S(1)}, f32[16,1,256]{2,1,0:T(1,128)S(1)}, u32[]{:S(2)}, u32[]{:S(2)}) collective-permute-start(f32[16,1,256]{2,1,0:T(1,128)S(1)} %get-tuple-element.40), channel_id=1, source_target_pairs={{0,16},{16,32},{32,48},{48,64},{64,80},{80,96},{96,112},{112,128},... | collective-permute-start | bytes 49160 | tf_op jit(solution)/shard_map/ppermute | solution.py:22
  193.3 5.1 %collective-permute-start.36 = (f32[16,16,256]{2,1,0:T(8,128)S(1)}, f32[16,16,256]{2,1,0:T(8,128)S(1)}, u32[]{:S(2)}, u32[]{:S(2)}) collective-permute-start(f32[16,16,256]{2,1,0:T(8,128)S(1)} %convolution_bitcast_fusion), channel_id=1, source_target_pairs={{0,16},{16,0},{32,48},{48,32},{64,80},{80,64},{96,112},{112,96},{1... | collective-permute-start | bytes 786440 | tf_op jit(solution)/shard_map/ppermute | solution.py:29
  201.5 8.5 %collective-permute-done.37 = f32[16,16,256]{2,1,0:T(8,128)S(1)} collective-permute-done((f32[16,16,256]{2,1,0:T(8,128)S(1)}, f32[16,16,256]{2,1,0:T(8,128)S(1)}, u32[]{:S(2)}, u32[]{:S(2)}) %collective-permute-start.37) | collective-permute-done | bytes 262176 | tf_op jit(solution)/shard_map/ppermute | solution.py:29
  212.0 9.2 %collective-permute-done.38 = f32[16,16,256]{2,1,0:T(8,128)S(1)} collective-permute-done((f32[16,16,256]{2,1,0:T(8,128)S(1)}, f32[16,16,256]{2,1,0:T(8,128)S(1)}, u32[]{:S(2)}, u32[]{:S(2)}) %collective-permute-start.38) | collective-permute-done | bytes 262176 | tf_op jit(solution)/shard_map/ppermute | solution.py:29
  224.8 5.3 %collective-permute-done.39 = f32[16,16,256]{2,1,0:T(8,128)S(1)} collective-permute-done((f32[16,16,256]{2,1,0:T(8,128)S(1)}, f32[16,16,256]{2,1,0:T(8,128)S(1)}, u32[]{:S(2)}, u32[]{:S(2)}) %collective-permute-start.39) | collective-permute-done | bytes 262176 | tf_op jit(solution)/shard_map/ppermute | solution.py:29
  230.1 4.6 %collective-permute-start.40 = (f32[16,16,256]{2,1,0:T(8,128)S(1)}, f32[16,16,256]{2,1,0:T(8,128)S(1)}, u32[]{:S(2)}, u32[]{:S(2)}) collective-permute-start(f32[16,16,256]{2,1,0:T(8,128)S(1)} %select_multiply_fusion.1), channel_id=1, source_target_pairs={{0,256},{16,272},{32,288},{48,304},{64,320},{80,336},{96,352},{112... | collective-permute-start | bytes 786440 | tf_op jit(solution)/shard_map/ppermute | solution.py:29
  234.8 5.1 %collective-permute-done.40 = f32[16,16,256]{2,1,0:T(8,128)S(1)} collective-permute-done((f32[16,16,256]{2,1,0:T(8,128)S(1)}, f32[16,16,256]{2,1,0:T(8,128)S(1)}, u32[]{:S(2)}, u32[]{:S(2)}) %collective-permute-start.40) | collective-permute-done | bytes 262176 | tf_op jit(solution)/shard_map/ppermute | solution.py:29
  241.9 54.6 %psum.7 = f32[16,16,16]{1,0,2:T(8,128)S(1)} all-reduce(f32[16,16,16]{1,0,2:T(8,128)S(1)} %select_bitcast_fusion), channel_id=1, replica_groups=mesh['gx'=32,'gy'=16] {'gy'}, use_global_device_ids=true, to_apply=%region_0.1 | all-reduce | flops 4096 | bytes 32768 | tf_op jit(solution)/shard_map/psum | solution.py:91
  (130 shorter events, 119.4 us)
Async XLA Ops:
  1.7 12.2 %collective-permute-start = (f32[16,1,256]{2,1,0:T(1,128)S(1)}, f32[16,1,256]{2,1,0:T(1,128)S(1)}, u32[]{:S(2)}, u32[]{:S(2)}) collective-permute-start(f32[16,1,256]{2,1,0:T(1,128)S(1)} %get-tuple-element.55), channel_id=1, source_target_pairs={{0,16},{16,32},{32,48},{48,64},{64,80},{80,96},{96,112},{112,128},... | collective-permute-start | bytes 49160 | tf_op jit(solution)/shard_map/ppermute | solution.py:22
  3.6 10.3 %collective-permute-start.1 = (f32[16,1,256]{2,1,0:T(1,128)S(1)}, f32[16,1,256]{2,1,0:T(1,128)S(1)}, u32[]{:S(2)}, u32[]{:S(2)}) collective-permute-start(f32[16,1,256]{2,1,0:T(1,128)S(1)} %get-tuple-element.54), channel_id=1, source_target_pairs={{16,0},{32,16},{48,32},{64,48},{80,64},{96,80},{112,96},{128,112},... | collective-permute-start | bytes 49160 | tf_op jit(solution)/shard_map/ppermute | solution.py:23
  8.3 12.0 %collective-permute-start.4 = (f32[16,1,256]{2,1,0:T(1,128)S(1)}, f32[16,1,256]{2,1,0:T(1,128)S(1)}, u32[]{:S(2)}, u32[]{:S(2)}) collective-permute-start(f32[16,1,256]{2,1,0:T(1,128)S(1)} %get-tuple-element.56), channel_id=1, source_target_pairs={{0,16},{16,32},{32,48},{48,64},{64,80},{80,96},{96,112},{112,128},... | collective-permute-start | bytes 49160 | tf_op jit(solution)/shard_map/ppermute | solution.py:22
  10.2 10.1 %collective-permute-start.5 = (f32[16,1,256]{2,1,0:T(1,128)S(1)}, f32[16,1,256]{2,1,0:T(1,128)S(1)}, u32[]{:S(2)}, u32[]{:S(2)}) collective-permute-start(f32[16,1,256]{2,1,0:T(1,128)S(1)} %get-tuple-element.57), channel_id=1, source_target_pairs={{16,0},{32,16},{48,32},{64,48},{80,64},{96,80},{112,96},{128,112},... | collective-permute-start | bytes 49160 | tf_op jit(solution)/shard_map/ppermute | solution.py:23
  15.0 11.3 %collective-permute-start.2 = (f32[16,18,1]{2,1,0:T(8,128)S(1)}, f32[16,18,1]{2,1,0:T(8,128)S(1)}, u32[]{:S(2)}, u32[]{:S(2)}) collective-permute-start(f32[16,18,1]{2,1,0:T(8,128)S(1)} %get-tuple-element.36), channel_id=1, source_target_pairs={{0,1},{1,2},{2,3},{3,4},{4,5},{5,6},{6,7},{7,8},{8,9},{9,10},{10,1... | collective-permute-start | bytes 3464 | tf_op jit(solution)/shard_map/ppermute | solution.py:22
  19.0 9.2 %collective-permute-start.3 = (f32[16,18,1]{2,1,0:T(8,128)S(1)}, f32[16,18,1]{2,1,0:T(8,128)S(1)}, u32[]{:S(2)}, u32[]{:S(2)}) collective-permute-start(f32[16,18,1]{2,1,0:T(8,128)S(1)} %get-tuple-element.37), channel_id=1, source_target_pairs={{1,0},{2,1},{3,2},{4,3},{5,4},{6,5},{7,6},{8,7},{9,8},{10,9},{11,1... | collective-permute-start | bytes 3464 | tf_op jit(solution)/shard_map/ppermute | solution.py:23
  20.5 9.5 %collective-permute-start.6 = (f32[16,18,1]{2,1,0:T(8,128)S(1)}, f32[16,18,1]{2,1,0:T(8,128)S(1)}, u32[]{:S(2)}, u32[]{:S(2)}) collective-permute-start(f32[16,18,1]{2,1,0:T(8,128)S(1)} %get-tuple-element.39), channel_id=1, source_target_pairs={{0,1},{1,2},{2,3},{3,4},{4,5},{5,6},{6,7},{7,8},{8,9},{9,10},{10,1... | collective-permute-start | bytes 3464 | tf_op jit(solution)/shard_map/ppermute | solution.py:22
  25.1 9.5 %collective-permute-start.7 = (f32[16,18,1]{2,1,0:T(8,128)S(1)}, f32[16,18,1]{2,1,0:T(8,128)S(1)}, u32[]{:S(2)}, u32[]{:S(2)}) collective-permute-start(f32[16,18,1]{2,1,0:T(8,128)S(1)} %get-tuple-element.38), channel_id=1, source_target_pairs={{1,0},{2,1},{3,2},{4,3},{5,4},{6,5},{7,6},{8,7},{9,8},{10,9},{11,1... | collective-permute-start | bytes 3464 | tf_op jit(solution)/shard_map/ppermute | solution.py:23
  44.1 8.0 %collective-permute-start.10 = (f32[16,18,1]{2,1,0:T(8,128)S(1)}, f32[16,18,1]{2,1,0:T(8,128)S(1)}, u32[]{:S(2)}, u32[]{:S(2)}) collective-permute-start(f32[16,18,1]{2,1,0:T(8,128)S(1)} %get-tuple-element.35), channel_id=1, source_target_pairs={{0,1},{1,2},{2,3},{3,4},{4,5},{5,6},{6,7},{7,8},{8,9},{9,10},{10,1... | collective-permute-start | bytes 3464 | tf_op jit(solution)/shard_map/ppermute | solution.py:22
  48.9 8.8 %collective-permute-start.11 = (f32[16,18,1]{2,1,0:T(8,128)S(1)}, f32[16,18,1]{2,1,0:T(8,128)S(1)}, u32[]{:S(2)}, u32[]{:S(2)}) collective-permute-start(f32[16,18,1]{2,1,0:T(8,128)S(1)} %get-tuple-element.34), channel_id=1, source_target_pairs={{1,0},{2,1},{3,2},{4,3},{5,4},{6,5},{7,6},{8,7},{9,8},{10,9},{11,1... | collective-permute-start | bytes 3464 | tf_op jit(solution)/shard_map/ppermute | solution.py:23
  58.7 7.3 %collective-permute-start.12 = (f32[16,1,256]{2,1,0:T(1,128)S(1)}, f32[16,1,256]{2,1,0:T(1,128)S(1)}, u32[]{:S(2)}, u32[]{:S(2)}) collective-permute-start(f32[16,1,256]{2,1,0:T(1,128)S(1)} %get-tuple-element.50), channel_id=1, source_target_pairs={{0,16},{16,32},{32,48},{48,64},{64,80},{80,96},{96,112},{112,128},... | collective-permute-start | bytes 49160 | tf_op jit(solution)/shard_map/ppermute | solution.py:22
  68.0 8.3 %collective-permute-start.14 = (f32[16,18,1]{2,1,0:T(8,128)S(1)}, f32[16,18,1]{2,1,0:T(8,128)S(1)}, u32[]{:S(2)}, u32[]{:S(2)}) collective-permute-start(f32[16,18,1]{2,1,0:T(8,128)S(1)} %get-tuple-element.33), channel_id=1, source_target_pairs={{0,1},{1,2},{2,3},{3,4},{4,5},{5,6},{6,7},{7,8},{8,9},{9,10},{10,1... | collective-permute-start | bytes 3464 | tf_op jit(solution)/shard_map/ppermute | solution.py:22
  73.1 7.6 %collective-permute-start.15 = (f32[16,18,1]{2,1,0:T(8,128)S(1)}, f32[16,18,1]{2,1,0:T(8,128)S(1)}, u32[]{:S(2)}, u32[]{:S(2)}) collective-permute-start(f32[16,18,1]{2,1,0:T(8,128)S(1)} %get-tuple-element.32), channel_id=1, source_target_pairs={{1,0},{2,1},{3,2},{4,3},{5,4},{6,5},{7,6},{8,7},{9,8},{10,9},{11,1... | collective-permute-start | bytes 3464 | tf_op jit(solution)/shard_map/ppermute | solution.py:23
  94.9 7.6 %collective-permute-start.19 = (f32[16,18,1]{2,1,0:T(8,128)S(1)}, f32[16,18,1]{2,1,0:T(8,128)S(1)}, u32[]{:S(2)}, u32[]{:S(2)}) collective-permute-start(f32[16,18,1]{2,1,0:T(8,128)S(1)} %get-tuple-element.30), channel_id=1, source_target_pairs={{1,0},{2,1},{3,2},{4,3},{5,4},{6,5},{7,6},{8,7},{9,8},{10,9},{11,1... | collective-permute-start | bytes 3464 | tf_op jit(solution)/shard_map/ppermute | solution.py:23
  112.8 7.9 %collective-permute-start.22 = (f32[16,18,1]{2,1,0:T(8,128)S(1)}, f32[16,18,1]{2,1,0:T(8,128)S(1)}, u32[]{:S(2)}, u32[]{:S(2)}) collective-permute-start(f32[16,18,1]{2,1,0:T(8,128)S(1)} %get-tuple-element.29), channel_id=1, source_target_pairs={{0,1},{1,2},{2,3},{3,4},{4,5},{5,6},{6,7},{7,8},{8,9},{9,10},{10,1... | collective-permute-start | bytes 3464 | tf_op jit(solution)/shard_map/ppermute | solution.py:22
  117.6 7.6 %collective-permute-start.23 = (f32[16,18,1]{2,1,0:T(8,128)S(1)}, f32[16,18,1]{2,1,0:T(8,128)S(1)}, u32[]{:S(2)}, u32[]{:S(2)}) collective-permute-start(f32[16,18,1]{2,1,0:T(8,128)S(1)} %get-tuple-element.28), channel_id=1, source_target_pairs={{1,0},{2,1},{3,2},{4,3},{5,4},{6,5},{7,6},{8,7},{9,8},{10,9},{11,1... | collective-permute-start | bytes 3464 | tf_op jit(solution)/shard_map/ppermute | solution.py:23
  135.4 8.3 %collective-permute-start.26 = (f32[16,18,1]{2,1,0:T(8,128)S(1)}, f32[16,18,1]{2,1,0:T(8,128)S(1)}, u32[]{:S(2)}, u32[]{:S(2)}) collective-permute-start(f32[16,18,1]{2,1,0:T(8,128)S(1)} %get-tuple-element.27), channel_id=1, source_target_pairs={{0,1},{1,2},{2,3},{3,4},{4,5},{5,6},{6,7},{7,8},{8,9},{9,10},{10,1... | collective-permute-start | bytes 3464 | tf_op jit(solution)/shard_map/ppermute | solution.py:22
  140.6 7.6 %collective-permute-start.27 = (f32[16,18,1]{2,1,0:T(8,128)S(1)}, f32[16,18,1]{2,1,0:T(8,128)S(1)}, u32[]{:S(2)}, u32[]{:S(2)}) collective-permute-start(f32[16,18,1]{2,1,0:T(8,128)S(1)} %get-tuple-element.26), channel_id=1, source_target_pairs={{1,0},{2,1},{3,2},{4,3},{5,4},{6,5},{7,6},{8,7},{9,8},{10,9},{11,1... | collective-permute-start | bytes 3464 | tf_op jit(solution)/shard_map/ppermute | solution.py:23
  162.4 7.6 %collective-permute-start.31 = (f32[16,18,1]{2,1,0:T(8,128)S(1)}, f32[16,18,1]{2,1,0:T(8,128)S(1)}, u32[]{:S(2)}, u32[]{:S(2)}) collective-permute-start(f32[16,18,1]{2,1,0:T(8,128)S(1)} %get-tuple-element.24), channel_id=1, source_target_pairs={{1,0},{2,1},{3,2},{4,3},{5,4},{6,5},{7,6},{8,7},{9,8},{10,9},{11,1... | collective-permute-start | bytes 3464 | tf_op jit(solution)/shard_map/ppermute | solution.py:23
  184.4 7.6 %collective-permute-start.35 = (f32[16,18,1]{2,1,0:T(8,128)S(1)}, f32[16,18,1]{2,1,0:T(8,128)S(1)}, u32[]{:S(2)}, u32[]{:S(2)}) collective-permute-start(f32[16,18,1]{2,1,0:T(8,128)S(1)} %get-tuple-element.22), channel_id=1, source_target_pairs={{1,0},{2,1},{3,2},{4,3},{5,4},{6,5},{7,6},{8,7},{9,8},{10,9},{11,1... | collective-permute-start | bytes 3464 | tf_op jit(solution)/shard_map/ppermute | solution.py:23
  199.6 10.5 %collective-permute-start.37 = (f32[16,16,256]{2,1,0:T(8,128)S(1)}, f32[16,16,256]{2,1,0:T(8,128)S(1)}, u32[]{:S(2)}, u32[]{:S(2)}) collective-permute-start(f32[16,16,256]{2,1,0:T(8,128)S(1)} %select_multiply_fusion.4), channel_id=1, source_target_pairs={{0,32},{16,48},{32,0},{48,16},{64,96},{80,112},{96,64},{112,80},{1... | collective-permute-start | bytes 786440 | tf_op jit(solution)/shard_map/ppermute | solution.py:29
  210.1 11.2 %collective-permute-start.38 = (f32[16,16,256]{2,1,0:T(8,128)S(1)}, f32[16,16,256]{2,1,0:T(8,128)S(1)}, u32[]{:S(2)}, u32[]{:S(2)}) collective-permute-start(f32[16,16,256]{2,1,0:T(8,128)S(1)} %select_multiply_fusion.3), channel_id=1, source_target_pairs={{0,64},{16,80},{32,96},{48,112},{64,0},{80,16},{96,32},{112,48},{1... | collective-permute-start | bytes 786440 | tf_op jit(solution)/shard_map/ppermute | solution.py:29
  221.3 8.8 %collective-permute-start.39 = (f32[16,16,256]{2,1,0:T(8,128)S(1)}, f32[16,16,256]{2,1,0:T(8,128)S(1)}, u32[]{:S(2)}, u32[]{:S(2)}) collective-permute-start(f32[16,16,256]{2,1,0:T(8,128)S(1)} %select_multiply_fusion.2), channel_id=1, source_target_pairs={{0,128},{16,144},{32,160},{48,176},{64,192},{80,208},{96,224},{112... | collective-permute-start | bytes 786440 | tf_op jit(solution)/shard_map/ppermute | solution.py:29
  230.1 9.8 %collective-permute-start.40 = (f32[16,16,256]{2,1,0:T(8,128)S(1)}, f32[16,16,256]{2,1,0:T(8,128)S(1)}, u32[]{:S(2)}, u32[]{:S(2)}) collective-permute-start(f32[16,16,256]{2,1,0:T(8,128)S(1)} %select_multiply_fusion.1), channel_id=1, source_target_pairs={{0,256},{16,272},{32,288},{48,304},{64,320},{80,336},{96,352},{112... | collective-permute-start | bytes 786440 | tf_op jit(solution)/shard_map/ppermute | solution.py:29
  (23 other events, 261.7 us)
where the time goes:
time: 299 us; the launch traced here: 297 us
  starting transfers between devices  129 us (43%)
  waiting for transfers between devices  95.6 us (32%)
  blocking collectives  54.6 us (18%)
  other arithmetic  11.4 us (4%)
  local copies, waits for them, and re-layouts  4.86 us (2%)
    ppermute x18, starting transfers between devices, extended(): before = lax.ppermute(last, axis, up)  77.8 us
    psum x1, blocking collectives, per_device(): sketch = lax.psum(picked, 'gy')  54.6 us
    ppermute x18, waiting for transfers between devices, extended(): after = lax.ppermute(leading, axis, down)  52 us
    ppermute x18, starting transfers between devices, extended(): after = lax.ppermute(leading, axis, down)  34.2 us
    ppermute x5, waiting for transfers between devices, partner_2(): lax.ppermute(array, axis, [(i, i ^ 1 << stride) for i in range(lax.axis_s...  29.3 us
    ppermute x5, starting transfers between devices, partner_2(): lax.ppermute(array, axis, [(i, i ^ 1 << stride) for i in range(lax.axis_s...  16.9 us
    ppermute x18, waiting for transfers between devices, extended(): before = lax.ppermute(last, axis, up)  14.3 us
  transfers between devices with their start and end apart: 41, of which 29 were waited for; matrix products, arithmetic and copies ran while one was open for 1% of the time, Pallas kernels for 0%

commit v1 on v0

v1 whole, which is shorter than its diff:
```python
import functools

import jax
import jax.numpy as jnp
import numpy as np
from jax import lax
from jax.experimental import pallas as pl
from jax.experimental.pallas import tpu as pltpu
from jax.sharding import PartitionSpec as P

SWEEPS = 8
HALO = SWEEPS
REACTION = 0.5
LOWEST = 0.5
HIGHEST = 62.0
MESH = pl.DeviceIdType.MESH
F32 = jnp.float32
BF16 = jnp.bfloat16


def split_bf16(x):
    high = x.astype(BF16)
    return high, (x - high.astype(F32)).astype(BF16)


def dot_nt(a, b):
    return lax.dot_general(a, b, (((1,), (1,)), ((), ())), preferred_element_type=F32)


def kernel(
    n_gx, n_gy,
    basis_hbm, kappa_hbm, sign_hbm, cols_hbm, mix_hbm,
    prec_hbm, image_hbm, sketch_hbm,
    in_u, in_k, in_sign, in_cols, in_mix,
    halo_u, halo_k, pack, strips,
    kap, fx, fy, fz, diag, res, dirn, prec, img, flip,
    out_p, out_i, pick, recv_1, part, recv_2, recv_3, out_s,
    load_sem, store_sem, row_send, row_recv, strip_send, strip_recv, step_send, step_recv,
):
    depth, rows, cols = in_u.shape
    wide = cols + 128
    lo, hi = HALO, HALO + rows
    total = rows + 2 * HALO
    samples = out_s.shape[2]
    share = samples // n_gy
    gx, gy = lax.axis_index("gx"), lax.axis_index("gy")
    has_up, has_down = gx > 0, gx < n_gx - 1
    has_left, has_right = gy > 0, gy < n_gy - 1

    loads = [
        pltpu.make_async_copy(src, dst, load_sem.at[i])
        for i, (src, dst) in enumerate(
            ((basis_hbm, in_u), (kappa_hbm, in_k), (sign_hbm, in_sign), (cols_hbm, in_cols), (mix_hbm, in_mix))
        )
    ]
    for load in loads:
        load.start()

    barrier = pltpu.get_barrier_semaphore()

    def greet(x, y):
        pl.semaphore_signal(barrier, inc=1, device_id=(x, y), device_id_type=MESH)

    def greet_col(t, c):
        greet(gx, lax.rem(gy + t, n_gy))
        return c

    def greet_row(t, c):
        greet(lax.rem(gx + t, n_gx), gy)
        return c

    lax.fori_loop(1, n_gy, greet_col, 0)
    lax.fori_loop(1, n_gx, greet_row, 0)
    vertical = ((-1, has_up), (1, has_down))
    sideways = ((-1, has_left), (1, has_right))
    for dx, ok_x in vertical:
        for dy, ok_y in sideways:
            @pl.when(ok_x & ok_y)
            def _():
                greet(gx + dx, gy + dy)
    n_diag = (has_up.astype(jnp.int32) + has_down.astype(jnp.int32)) * (
        has_left.astype(jnp.int32) + has_right.astype(jnp.int32)
    )

    def row_copy(array, k):
        source, target = ((in_u, halo_u), (in_k, halo_k))[array]
        first = rows - HALO if k == 0 else 0
        return pltpu.make_async_remote_copy(
            src_ref=source.at[:, pl.ds(first, HALO), :],
            dst_ref=target.at[k],
            send_sem=row_send.at[array, k],
            recv_sem=row_recv.at[array, k],
            device_id=(gx + (1 if k == 0 else -1), gy),
            device_id_type=MESH,
        )

    def strip_copy(side, dx):
        return pltpu.make_async_remote_copy(
            src_ref=pack.at[side],
            dst_ref=strips.at[side, 1 - dx],
            send_sem=strip_send.at[side, 1 - dx],
            recv_sem=strip_recv.at[side, 1 - dx],
            device_id=(gx + dx, gy + (1 if side == 0 else -1)),
            device_id_type=MESH,
        )

    loads[0].wait()
    loads[1].wait()
    pl.semaphore_wait(barrier, n_gx + n_gy - 2 + n_diag)
    send_ok = (has_down, has_up)
    recv_ok = (has_up, has_down)
    for k in range(2):
        @pl.when(send_ok[k])
        def _():
            row_copy(1, k).start()
            row_copy(0, k).start()

    lane = lax.broadcasted_iota(jnp.int32, (depth, 128), 1)
    for half in range(rows // 8):
        for source, target in ((in_u, res), (in_k, kap)):
            block = source[:, 8 * half:8 * half + 8, :]
            target[lo + 8 * half:lo + 8 * half + 8, :, 0:cols] = jnp.swapaxes(block, 0, 1)
    for array, source in enumerate((res, kap)):
        left = jnp.zeros((depth, 128), F32)
        right = jnp.zeros((depth, 128), F32)
        for i in range(rows):
            here = (lane >= 8 * i) & (lane < 8 * i + 8)
            right = jnp.where(here, pltpu.roll(source[lo + i, :, cols - 128:cols], (8 * i + 8) % 128, 1), right)
            first = source[lo + i, :, 0:128]
            left = jnp.where(here, pltpu.roll(first, 8 * i, 1) if i else first, left)
        pack[0, array] = right
        pack[1, array] = left

    side_ok = (has_right, has_left)
    for side in range(2):
        for dx in (0, -1, 1):
            ok = side_ok[side]
            if dx:
                ok = ok & (has_up if dx < 0 else has_down)

            @pl.when(ok)
            def _():
                strip_copy(side, dx).start()

    for k in range(2):
        @pl.when(jnp.logical_not(recv_ok[k]))
        def _():
            halo_u[k] = jnp.zeros(halo_u.shape[1:], F32)
            halo_k[k] = jnp.zeros(halo_k.shape[1:], F32)
    from_ok = (has_left, has_right)
    arrives = {}
    for side in range(2):
        for dx in (0, -1, 1):
            ok = from_ok[side]
            if dx:
                ok = ok & (has_up if dx > 0 else has_down)
            arrives[side, dx] = ok

            @pl.when(jnp.logical_not(ok))
            def _():
                strips[side, 1 - dx] = jnp.zeros(strips.shape[2:], F32)

    loads[3].wait()
    s_of = lax.broadcasted_iota(jnp.int32, (samples, cols), 0)
    c_of = lax.broadcasted_iota(jnp.int32, (samples, cols), 1)
    wanted = jnp.zeros((samples, cols), jnp.int32)
    for s in range(samples):
        wanted = jnp.where(s_of == s, in_cols[s], wanted)
    select = jnp.where(wanted == c_of, 1.0, 0.0).astype(BF16)

    for side in range(2):
        for dx in (0, -1, 1):
            @pl.when(arrives[side, dx])
            def _():
                strip_copy(side, dx).wait_recv()

    def ring(array, slot, packed_row):
        before = pltpu.roll(strips[0, slot, array], (120 - 8 * packed_row) % 128, 1)
        after = strips[1, slot, array]
        if packed_row:
            after = pltpu.roll(after, (128 - 8 * packed_row) % 128, 1)
        return jnp.where(lane < 8, after, jnp.where(lane >= 120, before, 0.0))

    for i in range(total):
        slot, packed_row = (0, rows - HALO + i) if i < lo else (1, i - lo) if i < hi else (2, i - hi)
        res[i, :, cols:wide] = ring(0, slot, packed_row)
        kap[i, :, cols:wide] = ring(1, slot, packed_row)

    for k in range(2):
        @pl.when(recv_ok[k])
        def _():
            row_copy(1, k).wait_recv()
            row_copy(0, k).wait_recv()
        first = 0 if k == 0 else hi
        for source, target in ((halo_u, res), (halo_k, kap)):
            target[first:first + HALO, :, 0:cols] = jnp.swapaxes(source[k], 0, 1)

    middle = (HIGHEST + LOWEST) / 2.0
    spread = (HIGHEST - LOWEST) / 2.0
    ratio = middle / spread
    d_of = lax.broadcasted_iota(jnp.int32, (depth, wide), 0)
    l_of = lax.broadcasted_iota(jnp.int32, (depth, wide), 1)
    at_left, at_right = gy == 0, gy == n_gy - 1
    outer_left = (l_of == 0) & at_left
    outer_right = (l_of == cols) & at_right
    half_y = jnp.where(outer_left | outer_right, 0.0, 0.5)
    half_z = jnp.where(d_of == 0, 0.0, 0.5)
    outer = (
        jnp.where((d_of == 0) | (d_of == depth - 1), 0.5, 0.0)
        + jnp.where(outer_left | ((l_of == cols - 1) & at_right), 0.5, 0.0)
    )

    def coefficients(i, before):
        here = kap[i]
        shut = ((i == lo) & (gx == 0)) | ((i == hi) & (gx == n_gx - 1))
        edge = ((i == lo) & (gx == 0)) | ((i == hi - 1) & (gx == n_gx - 1))
        fx[i] = jnp.where(shut, 0.0, 0.5) * (here + before)
        fy[i] = half_y * (here + pltpu.roll(here, 1, 1))
        fz[i] = half_z * (here + pltpu.roll(here, 1, 0))
        diag[i] = REACTION + (outer + jnp.where(edge, 0.5, 0.0)) * here
        dirn[i] = res[i] * (1.0 / middle)
        return here

    dirn[0] = res[0] * (1.0 / middle)
    lax.fori_loop(1, total, coefficients, kap[0])

    def applied(u, u_next, flux, face, i):
        flux_next = face * (u_next - u)
        flux_y = fy[i] * (u - pltpu.roll(u, 1, 1))
        flux_z = fz[i] * (u - pltpu.roll(u, 1, 0))
        out = diag[i] * u + (flux - flux_next)
        out = out + (flux_y - pltpu.roll(flux_y, wide - 1, 1))
        out = out + (flux_z - pltpu.roll(flux_z, depth - 1, 0))
        return out, flux_next

    rho = 1.0 / ratio
    for sweep in range(SWEEPS - 1):
        reach = HALO - 1 - sweep
        rho_next = 1.0 / (2.0 * ratio - rho)
        keep, gain = rho_next * rho, 2.0 * rho_next / spread
        rho = rho_next

        def row(i, carry, sweep=sweep, keep=keep, gain=gain):
            u, flux = carry
            u_next = dirn[i + 1]
            au, flux = applied(u, u_next, flux, fx[i + 1], i)
            left_over = res[i] - au
            res[i] = left_over
            new = keep * u + gain * left_over
            dirn[i] = new
            prec[i] = (u if sweep == 0 else prec[i]) + new
            return u_next, flux

        start = lo - reach
        u0 = dirn[start]
        lax.fori_loop(start, hi + reach, row, (u0, fx[start] * (u0 - dirn[start - 1])))

    for half in range(rows // 8):
        block = prec[lo + 8 * half:lo + 8 * half + 8, :, 0:cols]
        out_p[:, 8 * half:8 * half + 8, :] = jnp.swapaxes(block, 0, 1)
    store_p = pltpu.make_async_copy(out_p, prec_hbm, store_sem.at[0])
    store_p.start()

    loads[2].wait()

    def last(i, carry):
        u, flux = carry
        u_next = prec[i + 1]
        au, flux = applied(u, u_next, flux, fx[i + 1], i)
        own = au[:, 0:cols]
        img[i - lo] = own
        flip[i - lo] = own * in_sign[pl.ds(i - lo, 1), :].astype(F32)
        return u_next, flux

    u0 = prec[lo]
    lax.fori_loop(lo, hi, last, (u0, fx[lo] * (u0 - prec[lo - 1])))

    high, low = split_bf16(flip[...].reshape(rows * depth, cols))
    pick[...] = dot_nt(select, high) + dot_nt(select, low)

    def exchange(step, source, target, device):
        return pltpu.make_async_remote_copy(
            src_ref=source, dst_ref=target, send_sem=step_send.at[step], recv_sem=step_recv.at[step],
            device_id=device, device_id_type=MESH,
        )

    mine = pl.ds(gy * share, share)

    def scatter(t, c):
        peer = lax.rem(gy + t, n_gy)
        exchange(0, pick.at[pl.ds(peer * share, share)], recv_1.at[gy], (gx, peer)).start()
        return c

    lax.fori_loop(1, n_gy, scatter, 0)
    recv_1[gy] = pick[mine, :]

    for half in range(rows // 8):
        out_i[:, 8 * half:8 * half + 8, :] = jnp.swapaxes(img[8 * half:8 * half + 8], 0, 1)
    store_i = pltpu.make_async_copy(out_i, image_hbm, store_sem.at[1])
    store_i.start()

    others_x, others_y = recv_2.at[pl.ds(0, n_gx - 1)], recv_1.at[pl.ds(0, n_gy - 1)]
    wait_1 = exchange(0, others_y, others_y, (gx, gy))
    wait_1.wait_recv()

    part[...] = jnp.sum(recv_1[...], axis=0)

    def gather_x(t, c):
        peer = lax.rem(gx + t, n_gx)
        exchange(1, part, recv_2.at[gx], (peer, gy)).start()
        return c

    lax.fori_loop(1, n_gx, gather_x, 0)
    recv_2[gx] = part[...]
    both = (lax.broadcasted_iota(jnp.int32, (n_gx, share, rows * depth), 0)) & gx
    parity = jnp.zeros_like(both)
    for bit in range(n_gx.bit_length() - 1):
        parity = parity ^ (both >> bit & 1)
    walsh = (1 - 2 * parity).astype(F32) * (1.0 / n_gx ** 0.5)
    wait_2 = exchange(1, others_x, others_x, (gx, gy))
    wait_2.wait_recv()
    recv_3[mine, :] = jnp.sum(recv_2[...] * walsh, axis=0)

    def gather_y(t, c):
        peer = lax.rem(gy + t, n_gy)
        exchange(2, recv_3.at[mine], recv_3.at[mine], (gx, peer)).start()
        return c

    lax.fori_loop(1, n_gy, gather_y, 0)
    loads[4].wait()
    wait_3 = exchange(2, others_y, others_y, (gx, gy))
    wait_3.wait_recv()
    high, low = split_bf16(recv_3[...])
    mixed = dot_nt(in_mix[0], high) + dot_nt(in_mix[0], low) + dot_nt(in_mix[1], high)
    out_s[...] = mixed.reshape(out_s.shape)
    store_s = pltpu.make_async_copy(out_s, sketch_hbm, store_sem.at[2])
    store_s.start()

    for k in range(2):
        @pl.when(send_ok[k])
        def _():
            row_copy(1, k).wait_send()
            row_copy(0, k).wait_send()
    for side in range(2):
        for dx in (0, -1, 1):
            ok = side_ok[side]
            if dx:
                ok = ok & (has_up if dx < 0 else has_down)

            @pl.when(ok)
            def _():
                strip_copy(side, dx).wait_send()
    wait_1.wait_send()
    wait_2.wait_send()
    wait_3.wait_send()
    store_p.wait()
    store_i.wait()
    store_s.wait()


def per_device(n_gx, n_gy, basis_vec, conductivity, sign_vals, sample_cols):
    depth, rows, cols = basis_vec.shape
    samples = sample_cols.shape[0]
    share = samples // n_gy
    wide, total = cols + 128, rows + 2 * HALO
    index = np.arange(rows)
    angle = (index[:, None] * index[None, :] % rows) * (2.0 * np.pi / rows)
    hartley = (np.cos(angle) + np.sin(angle)) / np.sqrt(rows)
    mix = np.einsum("jk,de->djke", hartley, np.eye(depth)).reshape(depth * rows, rows * depth).astype(np.float32)
    mix_high = mix.astype(jnp.bfloat16)
    mix_low = (mix - mix_high.astype(np.float32)).astype(jnp.bfloat16)
    mix = jnp.asarray(np.stack([mix_high, mix_low]))

    field = (depth, rows, cols)
    tall = pltpu.VMEM((total, depth, wide), F32)
    scratch = [
        pltpu.VMEM(field, F32), pltpu.VMEM(field, F32), pltpu.VMEM((rows, cols), jnp.int32),
        pltpu.SMEM((samples,), jnp.int32), pltpu.VMEM(mix.shape, BF16),
        pltpu.VMEM((2, depth, HALO, cols), F32), pltpu.VMEM((2, depth, HALO, cols), F32),
        pltpu.VMEM((2, 2, depth, 128), F32), pltpu.VMEM((2, 3, 2, depth, 128), F32),
        tall, tall, tall, tall, tall, tall, tall, tall,
        pltpu.VMEM((rows, depth, cols), F32), pltpu.VMEM((rows, depth, cols), F32),
        pltpu.VMEM(field, F32), pltpu.VMEM(field, F32),
        pltpu.VMEM((samples, rows * depth), F32), pltpu.VMEM((n_gy, share, rows * depth), F32),
        pltpu.VMEM((share, rows * depth), F32), pltpu.VMEM((n_gx, share, rows * depth), F32),
        pltpu.VMEM((samples, rows * depth), F32), pltpu.VMEM((depth, rows, samples), F32),
        pltpu.SemaphoreType.DMA((5,)), pltpu.SemaphoreType.DMA((3,)),
        pltpu.SemaphoreType.DMA((2, 2)), pltpu.SemaphoreType.DMA((2, 2)),
        pltpu.SemaphoreType.DMA((2, 3)), pltpu.SemaphoreType.DMA((2, 3)),
        pltpu.SemaphoreType.DMA((3,)), pltpu.SemaphoreType.DMA((3,)),
    ]
    return pl.pallas_call(
        functools.partial(kernel, n_gx, n_gy),
        out_shape=(
            jax.ShapeDtypeStruct(field, F32),
            jax.ShapeDtypeStruct(field, F32),
            jax.ShapeDtypeStruct((depth, rows, samples), F32),
        ),
        in_specs=[pl.BlockSpec(memory_space=pl.ANY)] * 5,
        out_specs=(pl.BlockSpec(memory_space=pl.ANY),) * 3,
        scratch_shapes=scratch,
        compiler_params=pltpu.CompilerParams(
            collective_id=0, has_side_effects=True, vmem_limit_bytes=32 * 1024 * 1024
        ),
    )(basis_vec, conductivity, sign_vals, sample_cols, mix)


def solution(mesh):
    in_specs = (P(None, "gx", "gy"), P(None, "gx", "gy"), P("gx", "gy"), P("gy"))
    out_specs = (P(None, "gx", "gy"), P(None, "gx", "gy"), P(None, "gx", None))
    return jax.shard_map(
        functools.partial(per_device, mesh.shape["gx"], mesh.shape["gy"]),
        mesh=mesh, in_specs=in_specs, out_specs=out_specs, check_vma=False,
    )
```

time: 299 us -> 79.9 us (0.27)
  the two profiles are of different devices: /device:TPU:24 before, /device:TPU:1 now
where the time goes in v1:
time: 79.9 us; the launch traced here: 79.6 us
  Pallas kernels  72.7 us (91%)
  local copies, waits for them, and re-layouts  6.28 us (8%)
    pallas_call x1, Pallas kernels, per_device(): pl.pallas_call(functools.partial(kernel, n_gx, n_gy), out_shape=(jax.Shap...  72.7 us
    unnamed x13, local copies, waits for them, and re-layouts  6.28 us

profile of v1, /device:TPU:1, one launch (start us, length us, event | category | flops | bytes accessed | tf_op | source)
XLA Modules:
  0.0 79.6 jit_solution(16972671151643247688)
XLA Ops:
  0.6 0.0 copy-start
  0.6 0.9 %copy-done = f32[16,16,256]{2,1,0:T(8,128)S(1)} copy-done((f32[16,16,256]{2,1,0:T(8,128)S(1)}, f32[16,16,256]{2,1,0:T(8,128)}, u32[]{:S(2)}) %copy-start) | copy-done | bytes 262168
  1.6 0.0 copy-start.1
  1.6 0.9 %copy-done.1 = f32[16,16,256]{2,1,0:T(8,128)S(1)} copy-done((f32[16,16,256]{2,1,0:T(8,128)S(1)}, f32[16,16,256]{2,1,0:T(8,128)}, u32[]{:S(2)}) %copy-start.1) | copy-done | bytes 262168
  2.5 0.0 copy-start.2
  2.5 0.9 %copy-done.2 = bf16[2,256,256]{2,1,0:T(8,128)(2,1)S(1)} copy-done((bf16[2,256,256]{2,1,0:T(8,128)(2,1)S(1)}, bf16[2,256,256]{2,1,0:T(8,128)(2,1)}, u32[]{:S(2)}) %copy-start.2) | copy-done | bytes 262168
  3.5 0.0 copy-start.3
  3.5 0.7 copy-done.3
  4.2 0.0 copy-start.4
  4.2 0.7 copy-done.4
  4.9 72.7 %shard_map.76 = (f32[16,16,256]{2,1,0:T(8,128)S(1)}, f32[16,16,256]{2,1,0:T(8,128)S(1)}, f32[16,16,16]{2,1,0:T(8,128)S(1)}) custom-call(f32[16,16,256]{2,1,0:T(8,128)S(1)} %copy-done, f32[16,16,256]{2,1,0:T(8,128)S(1)} %copy-done.1, s32[16,256]{1,0:T(8,128)S(1)} %copy-done.3, s32[16]{0:T(128)S(1)} %copy-done.4, bf16[2,256,256]{2,1,0:T(8,128)(2,1)S(1)} %copy-done.2), custom_call_target="tpu_custom_call" | custom-call | tf_op jit(solution)/shard_map/pallas_call | solution.py:392
  77.6 0.7 copy.11
  78.3 0.7 copy.12
  79.0 0.7 copy.13
Async XLA Ops:
  0.6 1.0 %copy-start = (f32[16,16,256]{2,1,0:T(8,128)S(1)}, f32[16,16,256]{2,1,0:T(8,128)}, u32[]{:S(2)}) copy-start(f32[16,16,256]{2,1,0:T(8,128)} %basis_hbm.1) | copy-start | bytes 786436
  1.6 0.9 %copy-start.1 = (f32[16,16,256]{2,1,0:T(8,128)S(1)}, f32[16,16,256]{2,1,0:T(8,128)}, u32[]{:S(2)}) copy-start(f32[16,16,256]{2,1,0:T(8,128)} %kappa_hbm.1) | copy-start | bytes 786436
  2.5 0.9 %copy-start.2 = (bf16[2,256,256]{2,1,0:T(8,128)(2,1)S(1)}, bf16[2,256,256]{2,1,0:T(8,128)(2,1)}, u32[]{:S(2)}) copy-start(bf16[2,256,256]{2,1,0:T(8,128)(2,1)} %constant.2.clone.mix_hbm) | copy-start | bytes 786436
  3.5 0.7 copy-start.3
  4.2 0.7 copy-start.4

commit v2 on v1

v2 whole, which is shorter than its diff:
```python
import functools

import jax
import jax.numpy as jnp
import numpy as np
from jax import lax
from jax.experimental import pallas as pl
from jax.experimental.pallas import tpu as pltpu
from jax.sharding import PartitionSpec as P

SWEEPS = 8
HALO = SWEEPS
REACTION = 0.5
LOWEST = 0.5
HIGHEST = 62.0
MESH = pl.DeviceIdType.MESH
F32 = jnp.float32
BF16 = jnp.bfloat16
COEF_ROWS = 5
COPIES = 4
SWEEP_ROWS = {30: 10, 28: 14, 26: 13, 24: 12, 22: 11, 20: 10, 18: 9}


def far_first(count):
    return sorted(range(1, count), key=lambda t: -min(t, count - t))


def far_in_plane(count):
    def hops(t):
        y, x = t // 2 % 4, t // 8
        return min(y, 4 - y) + min(x, 4 - x)
    return sorted(range(1, count), key=lambda t: -hops(t))


def split_bf16(x):
    high = x.astype(BF16)
    return high, (x - high.astype(F32)).astype(BF16)


def looped(first, end, count, body):
    steps = (end - first) // count

    def step(t, c):
        body(first + t * count, count)
        return c

    lax.fori_loop(0, steps, step, 0)
    if (end - first) % count:
        body(first + steps * count, (end - first) % count)


def dot_nt(a, b):
    return lax.dot_general(a, b, (((1,), (1,)), ((), ())), preferred_element_type=F32)


def kernel(
    n_gx, n_gy,
    basis_hbm, kappa_hbm, sign_hbm, cols_hbm, mix_hbm,
    out_p, out_i, out_s,
    in_u, in_k, in_sign, in_cols, in_mix,
    halo_u, halo_k, pack, strips,
    kap, fx, fy, fy2, fz, diag, base, prec_a, prec_b, img, flip,
    pick, recv_1, part, recv_2, recv_3,
    load_sem, row_send, row_recv, strip_send, strip_recv, step_send, step_recv, token_x, token_y,
):
    depth, rows, cols = in_u.shape
    wide = cols + 128
    lo, hi = HALO, HALO + rows
    total = rows + 2 * HALO
    samples = out_s.shape[2]
    pieces, share = recv_3.shape[0], recv_3.shape[1]
    gx, gy = lax.axis_index("gx"), lax.axis_index("gy")
    has_up, has_down = gx > 0, gx < n_gx - 1
    has_left, has_right = gy > 0, gy < n_gy - 1

    loads = [
        pltpu.make_async_copy(src, dst, load_sem.at[i])
        for i, (src, dst) in enumerate(
            ((basis_hbm, in_u), (kappa_hbm, in_k), (sign_hbm, in_sign), (cols_hbm, in_cols), (mix_hbm, in_mix))
        )
    ]
    for load in loads:
        load.start()

    barrier = pltpu.get_barrier_semaphore()

    def around_x(t):
        return lax.rem(gx + t + n_gx, n_gx), gy

    def around_y(t):
        return gx, lax.rem(gy + t + n_gy, n_gy)

    def tell(semaphore, device):
        pl.semaphore_signal(semaphore, inc=1, device_id=device, device_id_type=MESH)

    for t in (1, -1):
        tell(barrier, around_y(t))
        tell(barrier, around_x(t))
    vertical = ((-1, has_up), (1, has_down))
    sideways = ((-1, has_left), (1, has_right))
    for dx, ok_x in vertical:
        for dy, ok_y in sideways:
            @pl.when(ok_x & ok_y)
            def _():
                tell(barrier, (gx + dx, gy + dy))
    n_diag = (has_up.astype(jnp.int32) + has_down.astype(jnp.int32)) * (
        has_left.astype(jnp.int32) + has_right.astype(jnp.int32)
    )

    def token(round_no, action):
        distance = 1 << round_no
        for count, around, semaphores in ((n_gy, around_y, token_y), (n_gx, around_x, token_x)):
            if distance < count // 2:
                if action == "tell":
                    tell(semaphores.at[round_no], around(distance))
                    tell(semaphores.at[round_no], around(-distance))
                else:
                    pl.semaphore_wait(semaphores.at[round_no], 2)

    def row_copy(array, k):
        source, target = ((in_u, halo_u), (in_k, halo_k))[array]
        first = rows - HALO if k == 0 else 0
        return pltpu.make_async_remote_copy(
            src_ref=source.at[:, pl.ds(first, HALO), :],
            dst_ref=target.at[k],
            send_sem=row_send.at[array, k],
            recv_sem=row_recv.at[array, k],
            device_id=(gx + (1 if k == 0 else -1), gy),
            device_id_type=MESH,
        )

    def strip_copy(side, dx):
        return pltpu.make_async_remote_copy(
            src_ref=pack.at[side],
            dst_ref=strips.at[side, 1 - dx],
            send_sem=strip_send.at[side, 1 - dx],
            recv_sem=strip_recv.at[side, 1 - dx],
            device_id=(gx + dx, gy + (1 if side == 0 else -1)),
            device_id_type=MESH,
        )

    loads[0].wait()
    loads[1].wait()
    pl.semaphore_wait(barrier, 4 + n_diag)
    token(0, "tell")
    send_ok = (has_down, has_up)
    recv_ok = (has_up, has_down)
    for k in range(2):
        @pl.when(send_ok[k])
        def _():
            row_copy(1, k).start()
            row_copy(0, k).start()

    half_d = depth // 2

    def place(block, target, first):
        block = block.reshape(half_d, 2, 8, cols)
        for odd in range(2):
            target[first:first + 8, odd * half_d:(odd + 1) * half_d, 0:cols] = jnp.swapaxes(block[:, odd], 0, 1)

    def put_back(source, first, target, row0):
        for odd in range(2):
            block = jnp.swapaxes(source[first:first + 8, odd * half_d:(odd + 1) * half_d, 0:cols], 0, 1)
            for m in range(half_d):
                target[2 * m + odd, row0:row0 + 8, :] = block[m]

    lane = lax.broadcasted_iota(jnp.int32, (depth, 128), 1)
    for part_no in range(rows // 8):
        for source, target in ((in_u, base), (in_k, kap)):
            place(source[:, 8 * part_no:8 * part_no + 8, :], target, lo + 8 * part_no)
    for array, source in enumerate((base, kap)):
        left = jnp.zeros((depth, 128), F32)
        right = jnp.zeros((depth, 128), F32)
        for i in range(rows):
            here = (lane >= 8 * i) & (lane < 8 * i + 8)
            right = jnp.where(here, pltpu.roll(source[lo + i, :, cols - 128:cols], (8 * i + 8) % 128, 1), right)
            first = source[lo + i, :, 0:128]
            left = jnp.where(here, pltpu.roll(first, 8 * i, 1) if i else first, left)
        pack[0, array] = right
        pack[1, array] = left

    side_ok = (has_right, has_left)
    for side in range(2):
        for dx in (0, -1, 1):
            ok = side_ok[side]
            if dx:
                ok = ok & (has_up if dx < 0 else has_down)

            @pl.when(ok)
            def _():
                strip_copy(side, dx).start()

    for k in range(2):
        @pl.when(jnp.logical_not(recv_ok[k]))
        def _():
            halo_u[k] = jnp.zeros(halo_u.shape[1:], F32)
            halo_k[k] = jnp.zeros(halo_k.shape[1:], F32)
    from_ok = (has_left, has_right)
    arrives = {}
    for side in range(2):
        for dx in (0, -1, 1):
            ok = from_ok[side]
            if dx:
                ok = ok & (has_up if dx > 0 else has_down)
            arrives[side, dx] = ok

            @pl.when(jnp.logical_not(ok))
            def _():
                strips[side, 1 - dx] = jnp.zeros(strips.shape[2:], F32)

    loads[3].wait()
    s_of = lax.broadcasted_iota(jnp.int32, (samples, cols), 0)
    c_of = lax.broadcasted_iota(jnp.int32, (samples, cols), 1)
    wanted = jnp.zeros((samples, cols), jnp.int32)
    for s in range(samples):
        wanted = jnp.where(s_of == s, in_cols[s], wanted)
    select = jnp.where(wanted == c_of, 1.0, 0.0).astype(BF16)

    for side in range(2):
        for dx in (0, -1, 1):
            @pl.when(arrives[side, dx])
            def _():
                strip_copy(side, dx).wait_recv()

    token(0, "wait")
    token(1, "tell")

    def ring(array, slot, packed_row):
        before = pltpu.roll(strips[0, slot, array], (120 - 8 * packed_row) % 128, 1)
        after = strips[1, slot, array]
        if packed_row:
            after = pltpu.roll(after, (128 - 8 * packed_row) % 128, 1)
        return jnp.where(lane < 8, after, jnp.where(lane >= 120, before, 0.0))

    for i in range(total):
        slot, packed_row = (0, rows - HALO + i) if i < lo else (1, i - lo) if i < hi else (2, i - hi)
        base[i, :, cols:wide] = ring(0, slot, packed_row)
        kap[i, :, cols:wide] = ring(1, slot, packed_row)

    for k in range(2):
        @pl.when(recv_ok[k])
        def _():
            row_copy(1, k).wait_recv()
            row_copy(0, k).wait_recv()
        first = 0 if k == 0 else hi
        for source, target in ((halo_u, base), (halo_k, kap)):
            place(source[k], target, first)

    token(1, "wait")
    token(2, "tell")

    middle = (HIGHEST + LOWEST) / 2.0
    spread = (HIGHEST - LOWEST) / 2.0
    ratio = middle / spread
    p_of = lax.broadcasted_iota(jnp.int32, (depth, wide), 0)
    l_of = lax.broadcasted_iota(jnp.int32, (depth, wide), 1)
    at_left, at_right = gy == 0, gy == n_gy - 1
    face_0, face_1 = (l_of == 0) & at_left, (l_of == cols) & at_right
    half_y = jnp.where(face_0 | face_1, 0.0, 0.5)
    half_y2 = jnp.where(((l_of == wide - 1) & at_left) | ((l_of == cols - 1) & at_right), 0.0, 0.5)
    half_z = jnp.where(p_of[0:half_d] == half_d - 1, 0.0, 0.5)
    outer = (
        jnp.where((p_of == 0) | (p_of == depth - 1), 0.5, 0.0)
        + jnp.where(face_0 | ((l_of == cols - 1) & at_right), 0.5, 0.0)
    )

    def coefficients(first, count):
        before = kap[first - 1]
        for j in range(count):
            i = first + j
            here = kap[i]
            even, odd = here[0:half_d], here[half_d:depth]
            fx[i] = 0.5 * (here + before)
            fy[i] = half_y * (here + pltpu.roll(here, 1, 1))
            fy2[i] = half_y2 * (here + pltpu.roll(here, wide - 1, 1))
            fz[i, 0:half_d] = 0.5 * (even + odd)
            fz[i, half_d:depth] = half_z * (odd + pltpu.roll(even, half_d - 1, 0))
            diag[i] = REACTION + outer * here
            prec_a[i] = base[i] * (1.0 / middle)
            before = here

    looped(1, total - 1, COEF_ROWS, coefficients)
    fx[total - 1] = 0.5 * (kap[total - 1] + kap[total - 2])
    for i in (0, total - 1):
        prec_a[i] = base[i] * (1.0 / middle)
    for inner, face, ok in ((lo, lo, has_up), (hi - 1, hi, has_down)):
        @pl.when(jnp.logical_not(ok))
        def _():
            fx[face] = jnp.zeros((depth, wide), F32)
            diag[inner] = diag[inner] + 0.5 * kap[inner]

    def applied(source, i, count):
        u = [source[i + j] for j in range(-1, count + 1)]
        flux = [fx[i + j] * (u[j + 1] - u[j]) for j in range(count + 1)]
        for j in range(count):
            here = u[j + 1]
            left = fy[i + j] * (here - pltpu.roll(here, 1, 1))
            right = fy2[i + j] * (pltpu.roll(here, wide - 1, 1) - here)
            out = diag[i + j] * here + (flux[j] - flux[j + 1])
            out = out + (left - right)
            even, odd = here[0:half_d], here[half_d:depth]
            inside = fz[i + j, 0:half_d] * (odd - even)
            between = fz[i + j, half_d:depth] * (pltpu.roll(even, half_d - 1, 0) - odd)
            out_even = out[0:half_d] + (pltpu.roll(between, 1, 0) - inside)
            out_odd = out[half_d:depth] + (inside - between)
            yield j, here, jnp.concatenate([out_even, out_odd], axis=0)

    rho = 1.0 / ratio
    buffers = (prec_a, prec_b)
    for sweep in range(SWEEPS - 1):
        reach = HALO - 1 - sweep
        rho_next = 1.0 / (2.0 * ratio - rho)
        keep, gain = rho_next * rho, 2.0 * rho_next / spread
        rho = rho_next
        source, target = buffers[sweep % 2], buffers[(sweep + 1) % 2]

        def advance(i, count, sweep=sweep, keep=keep, gain=gain, source=source, target=target):
            for j, here, au in applied(source, i, count):
                change = here if sweep == 0 else here - target[i + j]
                target[i + j] = (here + keep * change) + gain * (base[i + j] - au)

        looped(lo - reach, hi + reach, SWEEP_ROWS[rows + 2 * reach], advance)
        if sweep == 3:
            token(2, "wait")
            token(3, "tell")

    prec = buffers[(SWEEPS - 1) % 2]
    loads[2].wait()

    def last(i, count):
        for j, here, au in applied(prec, i, count):
            own = au[:, 0:cols]
            img[i - lo + j] = own
            flip[i - lo + j] = own * in_sign[pl.ds(i - lo + j, 1), :].astype(F32)

    looped(lo, hi, 8, last)

    high, low = split_bf16(flip[...].reshape(rows * depth, cols))
    picked = dot_nt(select, high) + dot_nt(select, low)
    for q in range(pieces):
        pick[q] = picked[q * share:(q + 1) * share]
    token(3, "wait")

    def exchange(step, source, target, device):
        return pltpu.make_async_remote_copy(
            src_ref=source, dst_ref=target, send_sem=step_send.at[step], recv_sem=step_recv.at[step],
            device_id=device, device_id_type=MESH,
        )

    for t in far_first(n_gy):
        peer = lax.rem(gy + t, n_gy)
        exchange(0, pick.at[lax.rem(peer, pieces)], recv_1.at[gy], (gx, peer)).start()
    mine = lax.rem(gy, pieces)
    recv_1[gy] = pick[mine]

    for part_no in range(rows // 8):
        put_back(img, 8 * part_no, out_i, 8 * part_no)
        put_back(prec, lo + 8 * part_no, out_p, 8 * part_no)

    others_x, others_y = recv_2.at[pl.ds(0, n_gx - 1)], recv_1.at[pl.ds(0, n_gy - 1)]
    wait_1 = exchange(0, others_y, others_y, (gx, gy))
    wait_1.wait_recv()
    part[...] = jnp.sum(recv_1[...], axis=0)

    for t in far_in_plane(n_gx):
        exchange(1, part, recv_2.at[gx], around_x(t)).start()
    recv_2[gx] = part[...]
    both = lax.broadcasted_iota(jnp.int32, (n_gx, share, rows * depth), 0) & gx
    parity = jnp.zeros_like(both)
    for bit in range(n_gx.bit_length() - 1):
        parity = parity ^ (both >> bit & 1)
    walsh = (1 - 2 * parity).astype(F32) * (1.0 / n_gx ** 0.5)
    wait_2 = exchange(1, others_x, others_x, (gx, gy))
    wait_2.wait_recv()
    recv_3[mine] = jnp.sum(recv_2[...] * walsh, axis=0)

    near = [t - pieces // 2 for t in range(pieces) if t != pieces // 2]
    for t in sorted(near, key=abs, reverse=True):
        exchange(2, recv_3.at[mine], recv_3.at[mine], around_y(t)).start()
    loads[4].wait()
    wait_3 = None
    if near:
        others_near = recv_1.at[pl.ds(0, pieces - 1)]
        wait_3 = exchange(2, others_near, others_near, (gx, gy))
        wait_3.wait_recv()
    high, low = split_bf16(jnp.concatenate([recv_3[q] for q in range(pieces)], axis=0))
    mixed = dot_nt(in_mix[0], high) + dot_nt(in_mix[0], low) + dot_nt(in_mix[1], high)
    out_s[...] = mixed.reshape(out_s.shape)

    for k in range(2):
        @pl.when(send_ok[k])
        def _():
            row_copy(1, k).wait_send()
            row_copy(0, k).wait_send()
    for side in range(2):
        for dx in (0, -1, 1):
            ok = side_ok[side]
            if dx:
                ok = ok & (has_up if dx < 0 else has_down)

            @pl.when(ok)
            def _():
                strip_copy(side, dx).wait_send()
    wait_1.wait_send()
    wait_2.wait_send()
    if wait_3 is not None:
        wait_3.wait_send()


def per_device(n_gx, n_gy, basis_vec, conductivity, sign_vals, sample_cols):
    depth, rows, cols = basis_vec.shape
    samples = sample_cols.shape[0]
    pieces = max(n_gy // COPIES, 1)
    share = samples // pieces
    wide, total = cols + 128, rows + 2 * HALO
    index = np.arange(rows)
    angle = (index[:, None] * index[None, :] % rows) * (2.0 * np.pi / rows)
    hartley = (np.cos(angle) + np.sin(angle)) / np.sqrt(rows)
    order = np.concatenate([np.arange(0, depth, 2), np.arange(1, depth, 2)])
    mix = np.einsum("jk,de->djke", hartley, np.eye(depth)[:, order]).reshape(depth * rows, rows * depth).astype(np.float32)
    mix_high = mix.astype(jnp.bfloat16)
    mix_low = (mix - mix_high.astype(np.float32)).astype(jnp.bfloat16)
    mix = jnp.asarray(np.stack([mix_high, mix_low]))

    field = (depth, rows, cols)
    tall = pltpu.VMEM((total, depth, wide), F32)
    scratch = [
        pltpu.VMEM(field, F32), pltpu.VMEM(field, F32), pltpu.VMEM((rows, cols), jnp.int32),
        pltpu.SMEM((samples,), jnp.int32), pltpu.VMEM(mix.shape, BF16),
        pltpu.VMEM((2, depth, HALO, cols), F32), pltpu.VMEM((2, depth, HALO, cols), F32),
        pltpu.VMEM((2, 2, depth, 128), F32), pltpu.VMEM((2, 3, 2, depth, 128), F32),
        tall, tall, tall, tall, tall, tall, tall, tall, tall,
        pltpu.VMEM((rows, depth, cols), F32), pltpu.VMEM((rows, depth, cols), F32),
        pltpu.VMEM((pieces, share, rows * depth), F32), pltpu.VMEM((n_gy, share, rows * depth), F32),
        pltpu.VMEM((share, rows * depth), F32), pltpu.VMEM((n_gx, share, rows * depth), F32),
        pltpu.VMEM((pieces, share, rows * depth), F32),
        pltpu.SemaphoreType.DMA((5,)),
        pltpu.SemaphoreType.DMA((2, 2)), pltpu.SemaphoreType.DMA((2, 2)),
        pltpu.SemaphoreType.DMA((2, 3)), pltpu.SemaphoreType.DMA((2, 3)),
        pltpu.SemaphoreType.DMA((3,)), pltpu.SemaphoreType.DMA((3,)),
        pltpu.SemaphoreType.REGULAR((4,)), pltpu.SemaphoreType.REGULAR((4,)),
    ]
    return pl.pallas_call(
        functools.partial(kernel, n_gx, n_gy),
        out_shape=(
            jax.ShapeDtypeStruct(field, F32),
            jax.ShapeDtypeStruct(field, F32),
            jax.ShapeDtypeStruct((depth, rows, samples), F32),
        ),
        in_specs=[pl.BlockSpec(memory_space=pltpu.HBM)] * 5,
        out_specs=(pl.BlockSpec(memory_space=pltpu.VMEM),) * 3,
        scratch_shapes=scratch,
        compiler_params=pltpu.CompilerParams(
            collective_id=0, has_side_effects=True, vmem_limit_bytes=59000 * 1024
        ),
    )(basis_vec, conductivity, sign_vals, sample_cols, mix)


def solution(mesh):
    in_specs = (P(None, "gx", "gy"), P(None, "gx", "gy"), P("gx", "gy"), P("gy"))
    out_specs = (P(None, "gx", "gy"), P(None, "gx", "gy"), P(None, "gx", None))
    return jax.shard_map(
        functools.partial(per_device, mesh.shape["gx"], mesh.shape["gy"]),
        mesh=mesh, in_specs=in_specs, out_specs=out_specs, check_vma=False,
    )
```

time: 79.9 us -> 46.7 us (0.58)
  Pallas kernels: 72.7 us -> 42.5 us
  local copies, waits for them, and re-layouts: 6.28 us -> 3.37 us
    pallas_call x1, Pallas kernels: 72.7 us -> 42.5 us  [per_device(): pl.pallas_call(functools.partial(kernel, n_gx, n_gy), out_shape=(jax.Shap...]
    unnamed x13 -> x7, local copies, waits for them, and re-layouts: 6.28 us -> 3.37 us
where the time goes in v2:
time: 46.7 us; the launch traced here: 46.5 us
  Pallas kernels  42.5 us (91%)
  local copies, waits for them, and re-layouts  3.37 us (7%)
  between operations  0.65 us (1%)
    pallas_call x1, Pallas kernels, per_device(): pl.pallas_call(functools.partial(kernel, n_gx, n_gy), out_shape=(jax.Shap...  42.5 us
    unnamed x7, local copies, waits for them, and re-layouts  3.37 us

profile of v2, /device:TPU:1, one launch (start us, length us, event | category | flops | bytes accessed | tf_op | source)
XLA Modules:
  0.0 46.5 jit_solution(3970611868078933956)
XLA Ops:
  0.6 42.5 %shard_map.76 = (f32[16,16,256]{2,1,0:T(8,128)}, f32[16,16,256]{2,1,0:T(8,128)}, f32[16,16,16]{2,1,0:T(8,128)}) custom-call(f32[16,16,256]{2,1,0:T(8,128)} %basis_hbm.1, f32[16,16,256]{2,1,0:T(8,128)} %kappa_hbm.1, s32[16,256]{1,0:T(8,128)} %sign_hbm.1, s32[16]{0:T(128)} %cols_hbm.1, bf16[2,256,256]{2,1,0:T(8,128)(2,1)} %constant.2.clone.mix_hbm), custom_call_target="tpu_custom_call" | custom-call | tf_op jit(solution)/shard_map/pallas_call | solution.py:443
  43.2 0.0 copy-start
  43.2 1.7 %copy.11 = f32[16,16,256]{2,1,0:T(8,128)} copy(f32[16,16,256]{2,1,0:T(8,128)} %get-tuple-element.6) | data formatting | bytes 524288
  44.9 0.0 copy-done
  44.9 0.0 copy-start.1
  44.9 0.7 %copy.12 = f32[16,16,256]{2,1,0:T(8,128)} copy(f32[16,16,256]{2,1,0:T(8,128)S(1)} %copy-done) | data formatting | bytes 524288
  45.6 0.3 copy-done.1
  45.9 0.7 %copy.13 = f32[16,16,16]{2,1,0:T(8,128)} copy(f32[16,16,16]{2,1,0:T(8,128)S(1)} %copy-done.1) | data formatting | bytes 32768
Async XLA Ops:
  43.2 1.7 %copy-start = (f32[16,16,256]{2,1,0:T(8,128)S(1)}, f32[16,16,256]{2,1,0:T(8,128)}, u32[]{:S(2)}) copy-start(f32[16,16,256]{2,1,0:T(8,128)} %get-tuple-element.7) | copy-start | bytes 786436
  44.9 1.0 %copy-start.1 = (f32[16,16,16]{2,1,0:T(8,128)S(1)}, f32[16,16,16]{2,1,0:T(8,128)}, u32[]{:S(2)}) copy-start(f32[16,16,16]{2,1,0:T(8,128)} %get-tuple-element.8) | copy-start | bytes 49156

commit v3 on v2

--- a/solution.py
+++ b/solution.py
@@ -16,9 +16,8 @@
 MESH = pl.DeviceIdType.MESH
 F32 = jnp.float32
 BF16 = jnp.bfloat16
-COEF_ROWS = 5
 COPIES = 4
-SWEEP_ROWS = {30: 10, 28: 14, 26: 13, 24: 12, 22: 11, 20: 10, 18: 9}
+LAST_KIB = 59000
 
 
 def far_first(count):
@@ -56,12 +55,12 @@
 def kernel(
     n_gx, n_gy,
     basis_hbm, kappa_hbm, sign_hbm, cols_hbm, mix_hbm,
-    out_p, out_i, out_s,
+    prec_hbm, image_hbm, sketch_hbm,
     in_u, in_k, in_sign, in_cols, in_mix,
     halo_u, halo_k, pack, strips,
     kap, fx, fy, fy2, fz, diag, base, prec_a, prec_b, img, flip,
-    pick, recv_1, part, recv_2, recv_3,
-    load_sem, row_send, row_recv, strip_send, strip_recv, step_send, step_recv, token_x, token_y,
+    pick, recv_1, part, recv_2, recv_3, out_p, out_i, out_s,
+    load_sem, store_sem, row_send, row_recv, strip_send, strip_recv, step_send, step_recv, token_x, token_y,
 ):
     depth, rows, cols = in_u.shape
     wide = cols + 128
@@ -216,14 +215,11 @@
         wanted = jnp.where(s_of == s, in_cols[s], wanted)
     select = jnp.where(wanted == c_of, 1.0, 0.0).astype(BF16)
 
-    for side in range(2):
-        for dx in (0, -1, 1):
+    def strips_arrived(dx):
+        for side in range(2):
             @pl.when(arrives[side, dx])
             def _():
                 strip_copy(side, dx).wait_recv()
-
-    token(0, "wait")
-    token(1, "tell")
 
     def ring(array, slot, packed_row):
         before = pltpu.roll(strips[0, slot, array], (120 - 8 * packed_row) % 128, 1)
@@ -232,22 +228,10 @@
             after = pltpu.roll(after, (128 - 8 * packed_row) % 128, 1)
         return jnp.where(lane < 8, after, jnp.where(lane >= 120, before, 0.0))
 
-    for i in range(total):
-        slot, packed_row = (0, rows - HALO + i) if i < lo else (1, i - lo) if i < hi else (2, i - hi)
-        base[i, :, cols:wide] = ring(0, slot, packed_row)
-        kap[i, :, cols:wide] = ring(1, slot, packed_row)
-
-    for k in range(2):
-        @pl.when(recv_ok[k])
-        def _():
-            row_copy(1, k).wait_recv()
-            row_copy(0, k).wait_recv()
-        first = 0 if k == 0 else hi
-        for source, target in ((halo_u, base), (halo_k, kap)):
-            place(source[k], target, first)
-
-    token(1, "wait")
-    token(2, "tell")
+    def close_ring(first, count, slot, packed_row):
+        for j in range(count):
+            base[first + j, :, cols:wide] = ring(0, slot, packed_row + j)
+            kap[first + j, :, cols:wide] = ring(1, slot, packed_row + j)
 
     middle = (HIGHEST + LOWEST) / 2.0
     spread = (HIGHEST - LOWEST) / 2.0
@@ -264,30 +248,19 @@
         + jnp.where(face_0 | ((l_of == cols - 1) & at_right), 0.5, 0.0)
     )
 
+    def face(i):
+        fx[i] = 0.5 * (kap[i] + kap[i - 1])
+
     def coefficients(first, count):
-        before = kap[first - 1]
-        for j in range(count):
-            i = first + j
+        for i in range(first, first + count):
             here = kap[i]
             even, odd = here[0:half_d], here[half_d:depth]
-            fx[i] = 0.5 * (here + before)
             fy[i] = half_y * (here + pltpu.roll(here, 1, 1))
             fy2[i] = half_y2 * (here + pltpu.roll(here, wide - 1, 1))
             fz[i, 0:half_d] = 0.5 * (even + odd)
             fz[i, half_d:depth] = half_z * (odd + pltpu.roll(even, half_d - 1, 0))
             diag[i] = REACTION + outer * here
             prec_a[i] = base[i] * (1.0 / middle)
-            before = here
-
-    looped(1, total - 1, COEF_ROWS, coefficients)
-    fx[total - 1] = 0.5 * (kap[total - 1] + kap[total - 2])
-    for i in (0, total - 1):
-        prec_a[i] = base[i] * (1.0 / middle)
-    for inner, face, ok in ((lo, lo, has_up), (hi - 1, hi, has_down)):
-        @pl.when(jnp.logical_not(ok))
-        def _():
-            fx[face] = jnp.zeros((depth, wide), F32)
-            diag[inner] = diag[inner] + 0.5 * kap[inner]
 
     def applied(source, i, count):
         u = [source[i + j] for j in range(-1, count + 1)]
@@ -305,24 +278,56 @@
             out_odd = out[half_d:depth] + (inside - between)
             yield j, here, jnp.concatenate([out_even, out_odd], axis=0)
 
-    rho = 1.0 / ratio
     buffers = (prec_a, prec_b)
+
+    def advance(sweep, i, count):
+        keep, gain = weights[sweep]
+        source, target = buffers[sweep % 2], buffers[(sweep + 1) % 2]
+        for j, here, au in applied(source, i, count):
+            change = here if sweep == 0 else here - target[i + j]
+            target[i + j] = (here + keep * change) + gain * (base[i + j] - au)
+
+    weights, rho = [], 1.0 / ratio
     for sweep in range(SWEEPS - 1):
-        reach = HALO - 1 - sweep
         rho_next = 1.0 / (2.0 * ratio - rho)
-        keep, gain = rho_next * rho, 2.0 * rho_next / spread
+        weights.append((rho_next * rho, 2.0 * rho_next / spread))
         rho = rho_next
-        source, target = buffers[sweep % 2], buffers[(sweep + 1) % 2]
-
-        def advance(i, count, sweep=sweep, keep=keep, gain=gain, source=source, target=target):
-            for j, here, au in applied(source, i, count):
-                change = here if sweep == 0 else here - target[i + j]
-                target[i + j] = (here + keep * change) + gain * (base[i + j] - au)
-
-        looped(lo - reach, hi + reach, SWEEP_ROWS[rows + 2 * reach], advance)
-        if sweep == 3:
-            token(2, "wait")
-            token(3, "tell")
+
+    token(0, "wait")
+    token(1, "tell")
+    strips_arrived(0)
+    close_ring(lo, rows, 1, 0)
+    for i in range(lo + 1, hi):
+        face(i)
+    coefficients(lo, rows)
+    for sweep in range(SWEEPS - 1):
+        first, end = lo + 1 + sweep, hi - 1 - sweep
+        if first < end:
+            advance(sweep, first, end - first)
+    token(1, "wait")
+    token(2, "tell")
+
+    for k, dx, first, packed_row in ((0, 1, 0, rows - HALO), (1, -1, hi, 0)):
+        strips_arrived(dx)
+        close_ring(first, HALO, 1 - dx, packed_row)
+
+        @pl.when(recv_ok[k])
+        def _():
+            row_copy(1, k).wait_recv()
+            row_copy(0, k).wait_recv()
+        for source, target in ((halo_u, base), (halo_k, kap)):
+            place(source[k], target, first)
+        for i in range(max(first, 1), first + HALO + 1 - k):
+            face(i)
+        coefficients(first, HALO)
+    for inner, edge, ok in ((lo, lo, has_up), (hi - 1, hi, has_down)):
+        @pl.when(jnp.logical_not(ok))
+        def _():
+            fx[edge] = jnp.zeros((depth, wide), F32)
+            diag[inner] = diag[inner] + 0.5 * kap[inner]
+    for sweep in range(SWEEPS - 1):
+        advance(sweep, 1 + sweep, HALO)
+        advance(sweep, total - 1 - HALO - sweep, HALO)
 
     prec = buffers[(SWEEPS - 1) % 2]
     loads[2].wait()
@@ -339,7 +344,8 @@
     picked = dot_nt(select, high) + dot_nt(select, low)
     for q in range(pieces):
         pick[q] = picked[q * share:(q + 1) * share]
-    token(3, "wait")
+    token(2, "wait")
+    token(3, "tell")
 
     def exchange(step, source, target, device):
         return pltpu.make_async_remote_copy(
@@ -355,13 +361,21 @@
 
     for part_no in range(rows // 8):
         put_back(img, 8 * part_no, out_i, 8 * part_no)
+    for part_no in range(rows // 8):
         put_back(prec, lo + 8 * part_no, out_p, 8 * part_no)
+    stores = [
+        pltpu.make_async_copy(source, target, store_sem.at[i])
+        for i, (source, target) in enumerate(((out_i, image_hbm), (out_p, prec_hbm), (out_s, sketch_hbm)))
+    ]
+    stores[0].start()
+    stores[1].start()
 
     others_x, others_y = recv_2.at[pl.ds(0, n_gx - 1)], recv_1.at[pl.ds(0, n_gy - 1)]
     wait_1 = exchange(0, others_y, others_y, (gx, gy))
     wait_1.wait_recv()
     part[...] = jnp.sum(recv_1[...], axis=0)
 
+    token(3, "wait")
     for t in far_in_plane(n_gx):
         exchange(1, part, recv_2.at[gx], around_x(t)).start()
     recv_2[gx] = part[...]
@@ -386,6 +400,7 @@
     high, low = split_bf16(jnp.concatenate([recv_3[q] for q in range(pieces)], axis=0))
     mixed = dot_nt(in_mix[0], high) + dot_nt(in_mix[0], low) + dot_nt(in_mix[1], high)
     out_s[...] = mixed.reshape(out_s.shape)
+    stores[2].start()
 
     for k in range(2):
         @pl.when(send_ok[k])
@@ -405,6 +420,24 @@
     wait_2.wait_send()
     if wait_3 is not None:
         wait_3.wait_send()
+    for store in stores:
+        store.wait()
+
+
+def hand_on(prec, image, sketch, prec_out, image_out, sketch_out, held_p, held_i, held_s, load_sem, store_sem):
+    held = (held_p, held_i, held_s)
+    loads = [pltpu.make_async_copy(s, h, load_sem.at[i]) for i, (s, h) in enumerate(zip((prec, image, sketch), held))]
+    stores = [
+        pltpu.make_async_copy(h, t, store_sem.at[i])
+        for i, (h, t) in enumerate(zip(held, (prec_out, image_out, sketch_out)))
+    ]
+    for load in loads:
+        load.start()
+    for load, store in zip(loads, stores):
+        load.wait()
+        store.start()
+    for store in stores:
+        store.wait()
 
 
 def per_device(n_gx, n_gy, basis_vec, conductivity, sign_vals, sample_cols):
@@ -434,26 +467,36 @@
         pltpu.VMEM((pieces, share, rows * depth), F32), pltpu.VMEM((n_gy, share, rows * depth), F32),
         pltpu.VMEM((share, rows * depth), F32), pltpu.VMEM((n_gx, share, rows * depth), F32),
         pltpu.VMEM((pieces, share, rows * depth), F32),
-        pltpu.SemaphoreType.DMA((5,)),
+        pltpu.VMEM(field, F32), pltpu.VMEM(field, F32), pltpu.VMEM((depth, rows, samples), F32),
+        pltpu.SemaphoreType.DMA((5,)), pltpu.SemaphoreType.DMA((3,)),
         pltpu.SemaphoreType.DMA((2, 2)), pltpu.SemaphoreType.DMA((2, 2)),
         pltpu.SemaphoreType.DMA((2, 3)), pltpu.SemaphoreType.DMA((2, 3)),
         pltpu.SemaphoreType.DMA((3,)), pltpu.SemaphoreType.DMA((3,)),
         pltpu.SemaphoreType.REGULAR((4,)), pltpu.SemaphoreType.REGULAR((4,)),
     ]
-    return pl.pallas_call(
+    results = pl.pallas_call(
         functools.partial(kernel, n_gx, n_gy),
         out_shape=(
             jax.ShapeDtypeStruct(field, F32),
             jax.ShapeDtypeStruct(field, F32),
             jax.ShapeDtypeStruct((depth, rows, samples), F32),
         ),
-        in_specs=[pl.BlockSpec(memory_space=pltpu.HBM)] * 5,
-        out_specs=(pl.BlockSpec(memory_space=pltpu.VMEM),) * 3,
+        in_specs=[pl.BlockSpec(memory_space=pl.ANY)] * 5,
+        out_specs=(pl.BlockSpec(memory_space=pl.ANY),) * 3,
         scratch_shapes=scratch,
         compiler_params=pltpu.CompilerParams(
             collective_id=0, has_side_effects=True, vmem_limit_bytes=59000 * 1024
         ),
     )(basis_vec, conductivity, sign_vals, sample_cols, mix)
+    return pl.pallas_call(
+        hand_on,
+        out_shape=tuple(jax.ShapeDtypeStruct(r.shape, F32) for r in results),
+        in_specs=[pl.BlockSpec(memory_space=pl.ANY)] * 3,
+        out_specs=(pl.BlockSpec(memory_space=pl.ANY),) * 3,
+        scratch_shapes=[pltpu.VMEM(r.shape, F32) for r in results]
+        + [pltpu.SemaphoreType.DMA((3,)), pltpu.SemaphoreType.DMA((3,))],
+        compiler_params=pltpu.CompilerParams(vmem_limit_bytes=LAST_KIB * 1024),
+    )(*results)
 
 
 def solution(mesh):

time: 46.7 us -> 41.4 us (0.89)
  local copies, waits for them, and re-layouts: 3.37 us -> 0 us
  Pallas kernels: 42.5 us -> 40.6 us
    pallas_call x1, Pallas kernels: 42.5 us -> 38.8 us  [per_device(): pl.pallas_call(functools.partial(kernel, n_gx, n_gy), out_shape=(jax.Shap...]
    unnamed x7 -> x0, local copies, waits for them, and re-layouts: 3.37 us -> none
    pallas_call x0 -> x1, Pallas kernels: none -> 1.83 us  [per_device(): pl.pallas_call(hand_on, out_shape=tuple((jax.ShapeDtypeStruct(r.shape, F3...]
where the time goes in v3:
time: 41.4 us; the launch traced here: 41.3 us
  Pallas kernels  40.6 us (98%)
  between operations  0.64 us (2%)
    pallas_call x1, Pallas kernels, per_device(): pl.pallas_call(functools.partial(kernel, n_gx, n_gy), out_shape=(jax.Shap...  38.8 us
    pallas_call x1, Pallas kernels, per_device(): pl.pallas_call(hand_on, out_shape=tuple((jax.ShapeDtypeStruct(r.shape, F3...  1.83 us

profile of v3, /device:TPU:1, one launch (start us, length us, event | category | flops | bytes accessed | tf_op | source)
XLA Modules:
  0.0 41.3 jit_solution(14922130912191968228)
XLA Ops:
  0.6 38.8 %shard_map.76 = (f32[16,16,256]{2,1,0:T(8,128)}, f32[16,16,256]{2,1,0:T(8,128)}, f32[16,16,16]{2,1,0:T(8,128)}) custom-call(f32[16,16,256]{2,1,0:T(8,128)} %basis_hbm.1, f32[16,16,256]{2,1,0:T(8,128)} %kappa_hbm.1, s32[16,256]{1,0:T(8,128)} %sign_hbm.1, s32[16]{0:T(128)} %cols_hbm.1, bf16[2,256,256]{2,1,0:T(8,128)(2,1)} %constant.2.clone.mix_hbm), custom_call_target="tpu_custom_call" | custom-call | tf_op jit(solution)/shard_map/pallas_call | solution.py:477
  39.4 1.8 %shard_map.77 = (f32[16,16,256]{2,1,0:T(8,128)}, f32[16,16,256]{2,1,0:T(8,128)}, f32[16,16,16]{2,1,0:T(8,128)}) custom-call(f32[16,16,256]{2,1,0:T(8,128)} %get-tuple-element.6.prec, f32[16,16,256]{2,1,0:T(8,128)} %get-tuple-element.7.image, f32[16,16,16]{2,1,0:T(8,128)} %get-tuple-element.8.sketch), custom_call_target="tpu_custom_call" | custom-call | tf_op jit(solution)/shard_map/pallas_call | solution.py:491

commit v4 on v3

--- a/solution.py
+++ b/solution.py
@@ -34,18 +34,6 @@
 def split_bf16(x):
     high = x.astype(BF16)
     return high, (x - high.astype(F32)).astype(BF16)
-
-
-def looped(first, end, count, body):
-    steps = (end - first) // count
-
-    def step(t, c):
-        body(first + t * count, count)
-        return c
-
-    lax.fori_loop(0, steps, step, 0)
-    if (end - first) % count:
-        body(first + steps * count, (end - first) % count)
 
 
 def dot_nt(a, b):
@@ -106,15 +94,17 @@
         has_left.astype(jnp.int32) + has_right.astype(jnp.int32)
     )
 
-    def token(round_no, action):
+    rings = {"x": (n_gx, around_x, token_x), "y": (n_gy, around_y, token_y)}
+
+    def token(ring_name, round_no, action):
+        count, around, semaphores = rings[ring_name]
         distance = 1 << round_no
-        for count, around, semaphores in ((n_gy, around_y, token_y), (n_gx, around_x, token_x)):
-            if distance < count // 2:
-                if action == "tell":
-                    tell(semaphores.at[round_no], around(distance))
-                    tell(semaphores.at[round_no], around(-distance))
-                else:
-                    pl.semaphore_wait(semaphores.at[round_no], 2)
+        if distance < count // 2:
+            if action == "tell":
+                tell(semaphores.at[round_no], around(distance))
+                tell(semaphores.at[round_no], around(-distance))
+            else:
+                pl.semaphore_wait(semaphores.at[round_no], 2)
 
     def row_copy(array, k):
         source, target = ((in_u, halo_u), (in_k, halo_k))[array]
@@ -140,16 +130,6 @@
 
     loads[0].wait()
     loads[1].wait()
-    pl.semaphore_wait(barrier, 4 + n_diag)
-    token(0, "tell")
-    send_ok = (has_down, has_up)
-    recv_ok = (has_up, has_down)
-    for k in range(2):
-        @pl.when(send_ok[k])
-        def _():
-            row_copy(1, k).start()
-            row_copy(0, k).start()
-
     half_d = depth // 2
 
     def place(block, target, first):
@@ -178,6 +158,9 @@
         pack[0, array] = right
         pack[1, array] = left
 
+    pl.semaphore_wait(barrier, 4 + n_diag)
+    token("y", 0, "tell")
+    token("x", 0, "tell")
     side_ok = (has_right, has_left)
     for side in range(2):
         for dx in (0, -1, 1):
@@ -188,6 +171,14 @@
             @pl.when(ok)
             def _():
                 strip_copy(side, dx).start()
+
+    send_ok = (has_down, has_up)
+    recv_ok = (has_up, has_down)
+    for k in range(2):
+        @pl.when(send_ok[k])
+        def _():
+            row_copy(1, k).start()
+            row_copy(0, k).start()
 
     for k in range(2):
         @pl.when(jnp.logical_not(recv_ok[k]))
@@ -293,8 +284,8 @@
         weights.append((rho_next * rho, 2.0 * rho_next / spread))
         rho = rho_next
 
-    token(0, "wait")
-    token(1, "tell")
+    token("y", 0, "wait")
+    token("y", 1, "tell")
     strips_arrived(0)
     close_ring(lo, rows, 1, 0)
     for i in range(lo + 1, hi):
@@ -304,8 +295,10 @@
         first, end = lo + 1 + sweep, hi - 1 - sweep
         if first < end:
             advance(sweep, first, end - first)
-    token(1, "wait")
-    token(2, "tell")
+    token("y", 1, "wait")
+    token("y", 2, "tell")
+    token("x", 0, "wait")
+    token("x", 1, "tell")
 
     for k, dx, first, packed_row in ((0, 1, 0, rows - HALO), (1, -1, hi, 0)):
         strips_arrived(dx)
@@ -332,20 +325,19 @@
     prec = buffers[(SWEEPS - 1) % 2]
     loads[2].wait()
 
-    def last(i, count):
-        for j, here, au in applied(prec, i, count):
+    picked = []
+    for first in range(lo, hi, 8):
+        for j, here, au in applied(prec, first, 8):
+            i = first - lo + j
             own = au[:, 0:cols]
-            img[i - lo + j] = own
-            flip[i - lo + j] = own * in_sign[pl.ds(i - lo + j, 1), :].astype(F32)
-
-    looped(lo, hi, 8, last)
-
-    high, low = split_bf16(flip[...].reshape(rows * depth, cols))
-    picked = dot_nt(select, high) + dot_nt(select, low)
+            img[i] = own
+            flip[i] = own * in_sign[i:i + 1, :].astype(F32)
+        high, low = split_bf16(flip[first - lo:first - lo + 8].reshape(8 * depth, cols))
+        picked.append(dot_nt(select, high) + dot_nt(select, low))
+    picked = jnp.concatenate(picked, axis=1)
     for q in range(pieces):
         pick[q] = picked[q * share:(q + 1) * share]
-    token(2, "wait")
-    token(3, "tell")
+    token("y", 2, "wait")
 
     def exchange(step, source, target, device):
         return pltpu.make_async_remote_copy(
@@ -358,6 +350,8 @@
         exchange(0, pick.at[lax.rem(peer, pieces)], recv_1.at[gy], (gx, peer)).start()
     mine = lax.rem(gy, pieces)
     recv_1[gy] = pick[mine]
+    token("x", 1, "wait")
+    token("x", 2, "tell")
 
     for part_no in range(rows // 8):
         put_back(img, 8 * part_no, out_i, 8 * part_no)
@@ -370,12 +364,15 @@
     stores[0].start()
     stores[1].start()
 
+    token("x", 2, "wait")
+    token("x", 3, "tell")
+
     others_x, others_y = recv_2.at[pl.ds(0, n_gx - 1)], recv_1.at[pl.ds(0, n_gy - 1)]
     wait_1 = exchange(0, others_y, others_y, (gx, gy))
     wait_1.wait_recv()
     part[...] = jnp.sum(recv_1[...], axis=0)
 
-    token(3, "wait")
+    token("x", 3, "wait")
     for t in far_in_plane(n_gx):
         exchange(1, part, recv_2.at[gx], around_x(t)).start()
     recv_2[gx] = part[...]

time: 41.4 us -> 41.2 us (level)
  no operation moved by 1% of the time
where the time goes in v4:
time: 41.2 us; the launch traced here: 41 us
  Pallas kernels  40.4 us (98%)
  between operations  0.64 us (2%)
    pallas_call x1, Pallas kernels, per_device(): pl.pallas_call(functools.partial(kernel, n_gx, n_gy), out_shape=(jax.Shap...  38.6 us
    pallas_call x1, Pallas kernels, per_device(): pl.pallas_call(hand_on, out_shape=tuple((jax.ShapeDtypeStruct(r.shape, F3...  1.83 us

profile of v4, /device:TPU:1, one launch (start us, length us, event | category | flops | bytes accessed | tf_op | source)
XLA Modules:
  0.0 41.0 jit_solution(1651694868773540377)
XLA Ops:
  0.6 38.6 %shard_map.76 = (f32[16,16,256]{2,1,0:T(8,128)}, f32[16,16,256]{2,1,0:T(8,128)}, f32[16,16,16]{2,1,0:T(8,128)}) custom-call(f32[16,16,256]{2,1,0:T(8,128)} %basis_hbm.1, f32[16,16,256]{2,1,0:T(8,128)} %kappa_hbm.1, s32[16,256]{1,0:T(8,128)} %sign_hbm.1, s32[16]{0:T(128)} %cols_hbm.1, bf16[2,256,256]{2,1,0:T(8,128)(2,1)} %constant.2.clone.mix_hbm), custom_call_target="tpu_custom_call" | custom-call | tf_op jit(solution)/shard_map/pallas_call | solution.py:474
  39.2 1.8 %shard_map.77 = (f32[16,16,256]{2,1,0:T(8,128)}, f32[16,16,256]{2,1,0:T(8,128)}, f32[16,16,16]{2,1,0:T(8,128)}) custom-call(f32[16,16,256]{2,1,0:T(8,128)} %get-tuple-element.6.prec, f32[16,16,256]{2,1,0:T(8,128)} %get-tuple-element.7.image, f32[16,16,16]{2,1,0:T(8,128)} %get-tuple-element.8.sketch), custom_call_target="tpu_custom_call" | custom-call | tf_op jit(solution)/shard_map/pallas_call | solution.py:488

commit v5 on v4

--- a/solution.py
+++ b/solution.py
@@ -18,6 +18,7 @@
 BF16 = jnp.bfloat16
 COPIES = 4
 LAST_KIB = 59000
+HAND_ON_PARTS = 2
 
 
 def far_first(count):
@@ -422,12 +423,15 @@
 
 
 def hand_on(prec, image, sketch, prec_out, image_out, sketch_out, held_p, held_i, held_s, load_sem, store_sem):
-    held = (held_p, held_i, held_s)
-    loads = [pltpu.make_async_copy(s, h, load_sem.at[i]) for i, (s, h) in enumerate(zip((prec, image, sketch), held))]
-    stores = [
-        pltpu.make_async_copy(h, t, store_sem.at[i])
-        for i, (h, t) in enumerate(zip(held, (prec_out, image_out, sketch_out)))
-    ]
+    loads, stores = [], []
+    for part_no in range(HAND_ON_PARTS):
+        for i, (source, held, target) in enumerate(
+            ((sketch, held_s, sketch_out), (prec, held_p, prec_out), (image, held_i, image_out))
+        ):
+            size = held.shape[0] // HAND_ON_PARTS
+            some = pl.ds(part_no * size, size)
+            loads.append(pltpu.make_async_copy(source.at[some], held.at[some], load_sem.at[i, part_no]))
+            stores.append(pltpu.make_async_copy(held.at[some], target.at[some], store_sem.at[i, part_no]))
     for load in loads:
         load.start()
     for load, store in zip(loads, stores):
@@ -491,7 +495,7 @@
         in_specs=[pl.BlockSpec(memory_space=pl.ANY)] * 3,
         out_specs=(pl.BlockSpec(memory_space=pl.ANY),) * 3,
         scratch_shapes=[pltpu.VMEM(r.shape, F32) for r in results]
-        + [pltpu.SemaphoreType.DMA((3,)), pltpu.SemaphoreType.DMA((3,))],
+        + [pltpu.SemaphoreType.DMA((3, HAND_ON_PARTS)), pltpu.SemaphoreType.DMA((3, HAND_ON_PARTS))],
         compiler_params=pltpu.CompilerParams(vmem_limit_bytes=LAST_KIB * 1024),
     )(*results)
 

time: 41.2 us -> 41.3 us (level)
  no operation moved by 1% of the time
where the time goes in v5:
time: 41.3 us; the launch traced here: 41.1 us
  Pallas kernels  40.5 us (98%)
  between operations  0.64 us (2%)
    pallas_call x1, Pallas kernels, per_device(): pl.pallas_call(functools.partial(kernel, n_gx, n_gy), out_shape=(jax.Shap...  38.6 us
    pallas_call x1, Pallas kernels, per_device(): pl.pallas_call(hand_on, out_shape=tuple((jax.ShapeDtypeStruct(r.shape, F3...  1.92 us

profile of v5, /device:TPU:1, one launch (start us, length us, event | category | flops | bytes accessed | tf_op | source)
XLA Modules:
  0.0 41.1 jit_solution(9166957737225595682)
XLA Ops:
  0.6 38.6 %shard_map.76 = (f32[16,16,256]{2,1,0:T(8,128)}, f32[16,16,256]{2,1,0:T(8,128)}, f32[16,16,16]{2,1,0:T(8,128)}) custom-call(f32[16,16,256]{2,1,0:T(8,128)} %basis_hbm.1, f32[16,16,256]{2,1,0:T(8,128)} %kappa_hbm.1, s32[16,256]{1,0:T(8,128)} %sign_hbm.1, s32[16]{0:T(128)} %cols_hbm.1, bf16[2,256,256]{2,1,0:T(8,128)(2,1)} %constant.2.clone.mix_hbm), custom_call_target="tpu_custom_call" | custom-call | tf_op jit(solution)/shard_map/pallas_call | solution.py:478
  39.2 1.9 %shard_map.77 = (f32[16,16,256]{2,1,0:T(8,128)}, f32[16,16,256]{2,1,0:T(8,128)}, f32[16,16,16]{2,1,0:T(8,128)}) custom-call(f32[16,16,256]{2,1,0:T(8,128)} %get-tuple-element.6.prec, f32[16,16,256]{2,1,0:T(8,128)} %get-tuple-element.7.image, f32[16,16,16]{2,1,0:T(8,128)} %get-tuple-element.8.sketch), custom_call_target="tpu_custom_call" | custom-call | tf_op jit(solution)/shard_map/pallas_call | solution.py:492
